TPU v7x, 32 devices: a whole 2x2x4 slice. The times are simulated.
32 devices in a mesh: lm: 8 (over y, x, core), cam: 4 (over z).
Axes of the slice: x: 2, y: 2, z: 4, core: 2. Of those that a mesh axis runs over, the one named last changes fastest.
Arguments:
- panels: bfloat16 [64, 16, 64, 384], P(('lm', 'cam')), may hold values from -0.59765625 to 0.59765625
- curvature: float32 [3, 3, 8192], P(None, None, ('lm', 'cam')), as said below
- visible_blocks: int32 [64, 16], P(('lm', 'cam')), may hold values from 0 to 31, as said below
- counts: int32 [64], P(('lm', 'cam')), may hold values from 2 to 16
- camera_hessian: float32 [32, 64, 64], P('lm'), may hold values from -6 to 6
Outputs:
- reduced_system: float32 [2048, 2048], P('lm', 'cam')
Inputs may be any that keep to these rules, and one draw needn't show every extreme that they name: `visible_blocks`: the 16 ids of a tile are distinct and lie in a window of 16 consecutive camera blocks, counted cyclically. `curvature`: each landmark's block is symmetric and strictly diagonally dominant.
All inputs are finite; a program needn't handle non-finite values.
Results may differ from a plain program's by a relative error of at most 0.0003.
Values may be sent and summed in bfloat16 or wider, within the bound.
No kernel may reach another device: no remote copies, remote signals or barrier semaphores. Data moves between devices by JAX's collectives and lax.ppermute only.
A program may use at most 128 MiB of HBM per device.

v0:
```python
import jax
import jax.numpy as jnp
from jax import lax
from jax.sharding import PartitionSpec as P

CB = 64
LMB = 128
K = 16


def invert_three(matrix):
    entry = [[matrix[row_pos, col_pos] for col_pos in range(3)] for row_pos in range(3)]
    cofactor = [
        [
            entry[(row_pos + 1) % 3][(col_pos + 1) % 3]
            * entry[(row_pos + 2) % 3][(col_pos + 2) % 3]
            - entry[(row_pos + 1) % 3][(col_pos + 2) % 3]
            * entry[(row_pos + 2) % 3][(col_pos + 1) % 3]
            for col_pos in range(3)
        ]
        for row_pos in range(3)
    ]
    determ = (
        entry[0][0] * cofactor[0][0] + entry[0][1] * cofactor[0][1] + entry[0][2] * cofactor[0][2]
    )
    return jnp.stack(
        [
            jnp.stack([cofactor[col_pos][row_pos] / determ for col_pos in range(3)])
            for row_pos in range(3)
        ]
    )


def form_panel(block_panel, inverse):
    split = block_panel.astype(jnp.float32).reshape(block_panel.shape[:-1] + (3, LMB))
    pieces = []
    for target in range(3):
        pieces.append(
            split[..., 0, :] * inverse[0, target]
            + split[..., 1, :] * inverse[1, target]
            + split[..., 2, :] * inverse[2, target]
        )
    return jnp.stack(pieces, axis=-2).reshape(block_panel.shape)


def body(panels, curvature, visible_blocks, counts, camera_hessian):
    tiles_here = panels.shape[0]
    live = jnp.arange(K, dtype=jnp.int32)[None, :] < counts[:, None]
    masked = jnp.where(live[:, :, None, None], panels, jnp.zeros_like(panels))
    inverse = invert_three(curvature).reshape(3, 3, tiles_here, LMB)
    tile_inverse = jnp.transpose(inverse, (2, 0, 1, 3))
    row_blocks = camera_hessian.shape[0]
    row_count = row_blocks * CB
    total_blocks = row_blocks * lax.axis_size("lm")
    col_blocks = total_blocks // lax.axis_size("cam")
    col_count = col_blocks * CB
    width = 3 * LMB
    row_start = lax.axis_index("lm") * row_blocks
    all_inverse = lax.all_gather(tile_inverse, "lm", axis=0, tiled=True)
    start_total = jnp.zeros((row_count, total_blocks, CB), jnp.float32)
    piece_panels = lax.all_gather(masked, "lm", axis=0, tiled=True)
    piece_ids = lax.all_gather(visible_blocks, "lm", axis=0, tiled=True)

    def step(total, inputs):
        block_panel, block_inverse, block_ids = inputs
        formed = form_panel(block_panel, block_inverse)
        local = block_ids - row_start
        local = jnp.where((local >= 0) & (local < row_blocks), local, row_blocks)
        placed = jnp.zeros((row_blocks, CB, width), jnp.float32).at[local].set(formed, mode="drop")
        product = jnp.einsum(
            "rp,kcp->rkc",
            placed.reshape(row_count, width),
            block_panel.astype(jnp.float32),
            precision=lax.Precision.HIGHEST,
            preferred_element_type=jnp.float32,
        )
        return (total.at[:, block_ids].add(product), None)

    result, unused = lax.scan(step, start_total, (piece_panels, all_inverse, piece_ids))
    reduced = lax.psum_scatter(
        result.reshape(row_count, total_blocks * CB), "cam", scatter_dimension=1, tiled=True
    )
    first_row = lax.axis_index("lm") * row_blocks
    first_col = lax.axis_index("cam") * col_blocks
    hessian = jnp.zeros((row_count, col_count), jnp.float32)
    for row_pos in range(row_blocks):
        offset = first_row + row_pos - first_col
        inside = (offset >= 0) & (offset < col_blocks)
        block = jnp.where(inside, camera_hessian[row_pos], jnp.zeros_like(camera_hessian[row_pos]))
        column = jnp.clip(offset, 0, col_blocks - 1) * CB
        hessian = lax.dynamic_update_slice(hessian, block, (jnp.int32(row_pos * CB), column))
    return hessian - reduced


def solution(mesh):
    return jax.shard_map(
        body,
        mesh=mesh,
        in_specs=(
            P(("lm", "cam"), None, None, None),
            P(None, None, ("lm", "cam")),
            P(("lm", "cam"), None),
            P(("lm", "cam")),
            P("lm", None, None),
        ),
        out_specs=P("lm", "cam"),
        check_vma=False,
    )
```

profile of v0, /device:TPU:0, one launch (start us, length us, event | category | flops | bytes accessed | tf_op | source)
XLA Modules:
  0.0 449.1 jit_solution(6536945814803319293)
XLA Ops:
  7.3 2.8 broadcast_select_fusion
  10.2 10.3 %all-gather = s32[8,2,16]{2,1,0:T(2,128)S(1)} all-gather(s32[1,2,16]{2,1,0:T(2,128)S(1)} %bitcast.188), channel_id=1, replica_groups=mesh['lm'=8,'cam'=4] {'lm'}, dimensions={0}, use_global_device_ids=true | all-gather | bytes 1152 | tf_op jit(solution)/shard_map/all_gather | solution.py:62
  20.6 10.2 %all_gather.11 = f32[16,3,3,128]{3,2,1,0:T(4,128)} all-gather(f32[2,3,3,128]{3,2,1,0:T(4,128)S(1)} %maximum_bitcast_fusion), channel_id=1, replica_groups=mesh['lm'=8,'cam'=4] {'lm'}, dimensions={0}, use_global_device_ids=true | all-gather | bytes 82944 | tf_op jit(solution)/shard_map/all_gather | solution.py:59
  30.8 54.6 %all-gather.3.cloned.1.call-done = bf16[16,16,64,384]{3,2,1,0:T(8,128)(2,1)} async-done(((bf16[2,16,64,384]{3,2,1,0:T(8,128)(2,1)}), bf16[16,16,64,384]{3,2,1,0:T(8,128)(2,1)}) %all-gather.3.cloned.1.call-update) | async-done | bytes 12582928 | tf_op jit(solution)/shard_map/all_gather | solution.py:61
  87.0 309.1 %while.10 = (s32[]{:T(128)}, f32[256,32,64]{0,2,1:T(8,128)}, s32[16,16]{1,0:T(8,128)S(1)}, s32[]{:T(128)}, bf16[16,16,64,384]{3,2,1,0:T(8,128)(2,1)}, /*index=5*/f32[16,3,3,128]{3,2,1,0:T(4,128)}, s32[]{:T(128)}, f32[]{:T(128)}) while((s32[]{:T(128)}, f32[256,32,64]{0,2,1:T(8,128)}, s32[16,16]{1,0:T(8,128)S(1)}, s32[]{:T(128)}, ...), condition=%wide.region_3.4_spmd, body=%wide.region_0.3_spmd.sunk | while | flops 1211367552 | bytes 42229216 | solution.py:79
  87.7 2.5 dynamic-slice_convert_fusion.2
  90.2 2.5 reshape.1109
  92.7 2.6 multiply_add_fusion.4
  107.0 2.5 dynamic-slice_convert_fusion.2
  109.5 2.5 reshape.1109
  112.0 2.6 multiply_add_fusion.4
  126.3 2.5 dynamic-slice_convert_fusion.2
  128.8 2.5 reshape.1109
  131.3 2.6 multiply_add_fusion.4
  137.2 2.5 scatter_fusion
  145.7 2.5 dynamic-slice_convert_fusion.2
  148.1 2.5 reshape.1109
  150.6 2.6 multiply_add_fusion.4
  156.5 2.5 scatter_fusion
  165.0 2.5 dynamic-slice_convert_fusion.2
  167.4 2.5 reshape.1109
  169.9 2.6 multiply_add_fusion.4
  175.9 2.5 scatter_fusion
  184.3 2.5 dynamic-slice_convert_fusion.2
  186.8 2.5 reshape.1109
  189.3 2.6 multiply_add_fusion.4
  195.2 2.5 scatter_fusion
  203.6 2.5 dynamic-slice_convert_fusion.2
  206.1 2.5 reshape.1109
  208.6 2.6 multiply_add_fusion.4
  214.5 2.5 scatter_fusion
  222.9 2.5 dynamic-slice_convert_fusion.2
  225.4 2.5 reshape.1109
  227.9 2.6 multiply_add_fusion.4
  233.8 2.5 scatter_fusion
  242.3 2.5 dynamic-slice_convert_fusion.2
  244.7 2.5 reshape.1109
  247.2 2.6 multiply_add_fusion.4
  253.2 2.5 scatter_fusion
  261.6 2.5 dynamic-slice_convert_fusion.2
  264.1 2.5 reshape.1109
  266.6 2.6 multiply_add_fusion.4
  280.9 2.5 dynamic-slice_convert_fusion.2
  283.4 2.5 reshape.1109
  285.9 2.6 multiply_add_fusion.4
  300.2 2.5 dynamic-slice_convert_fusion.2
  302.7 2.5 reshape.1109
  305.2 2.6 multiply_add_fusion.4
  311.1 2.5 scatter_fusion
  319.5 2.5 dynamic-slice_convert_fusion.2
  322.0 2.5 reshape.1109
  324.5 2.6 multiply_add_fusion.4
  338.8 2.5 dynamic-slice_convert_fusion.2
  341.3 2.5 reshape.1109
  343.8 2.6 multiply_add_fusion.4
  349.7 2.5 scatter_fusion
  358.2 2.5 dynamic-slice_convert_fusion.2
  360.6 2.5 reshape.1109
  363.1 2.6 multiply_add_fusion.4
  377.5 2.5 dynamic-slice_convert_fusion.2
  379.9 2.5 reshape.1109
  382.4 2.6 multiply_add_fusion.4
  388.4 2.5 scatter_fusion
  402.0 38.2 %reduce-scatter.2.cloned.1.call-done = f32[256,512]{0,1:T(8,128)} async-done(((f32[256,2048]{0,1:T(8,128)}), f32[256,512]{0,1:T(8,128)}) %reduce-scatter.2.cloned.1.call-update) | async-done | bytes 524304 | tf_op jit(solution)/shard_map/reduce_scatter | solution.py:80
  (230 shorter events, 172.2 us)
Async XLA Ops:
  6.5 78.9 %all-gather.3.cloned.1.call-start = ((), (), s32[]{:S(2)}) async-start(), calls=%async_computation.1 | async-start | bytes 14155776 | tf_op jit(solution)/shard_map/all_gather | solution.py:61
  7.3 2.9 copy-start.4
  7.3 13.3 %copy-start.3 = (f32[3,3,256]{2,1,0:T(4,128)S(1)}, f32[3,3,256]{2,1,0:T(4,128)}, u32[]{:S(2)}) copy-start(f32[3,3,256]{2,1,0:T(4,128)} %param.8) | copy-start | bytes 27652
  10.1 430.0 %reduce-scatter.2.cloned.1.call-start = ((), (), s32[]{:S(2)}) async-start(), calls=%async_computation.2 | async-start | bytes 2621440 | tf_op jit(solution)/shard_map/reduce_scatter | solution.py:80
  101.1 2.3 copy-start
  105.0 1.3 copy-start.1
  120.4 2.3 copy-start
  124.3 1.3 copy-start.1
  139.7 2.3 copy-start
  143.6 1.3 copy-start.1
  159.0 2.3 copy-start
  163.0 1.3 copy-start.1
  178.3 2.3 copy-start
  182.3 1.3 copy-start.1
  197.7 2.3 copy-start
  201.6 1.3 copy-start.1
  217.0 2.3 copy-start
  220.9 1.3 copy-start.1
  236.3 2.3 copy-start
  240.2 1.3 copy-start.1
  255.6 2.3 copy-start
  259.6 1.3 copy-start.1
  274.9 2.3 copy-start
  278.9 1.3 copy-start.1
  294.3 2.3 copy-start
  298.2 1.3 copy-start.1
  313.6 2.3 copy-start
  317.5 1.3 copy-start.1
  332.9 2.3 copy-start
  336.8 1.3 copy-start.1
  352.2 2.3 copy-start
  356.1 1.3 copy-start.1
  371.5 2.3 copy-start
  375.5 1.3 copy-start.1
  390.8 2.3 copy-start
  394.8 1.3 copy-start.1
  396.1 0.9 copy-start.2
Sparse Core Ops, SparseCore 0:
  10.2 75.1 all-gather.2
  396.2 43.8 reduce-scatter.1
where the time goes:
time: 453 us; the launch traced here: 449 us
  local copies, waits for them, and re-layouts  149 us (33%)
  other arithmetic  135 us (30%)
  waiting for transfers between devices  92.8 us (20%)
  matrix products  36.7 us (8%)
  blocking collectives  20.6 us (5%)
  between operations  13.6 us (3%)
    all_gather x1, waiting for transfers between devices, body(): piece_panels = lax.all_gather(masked, 'lm', axis=0, tiled=True)  54.6 us
    add x16, other arithmetic, form_panel(): split[..., 0, :] * inverse[0, target]  41.9 us
    convert_element_type x16, local copies, waits for them, and re-layouts, form_panel(): block_panel.astype(jnp.float32).reshape(block_panel.shape[:-1] + (3, LMB))  39.9 us
    convert_element_type x16, other arithmetic, form_panel(): block_panel.astype(jnp.float32).reshape(block_panel.shape[:-1] + (3, LMB))  39.4 us
    scatter x16, local copies, waits for them, and re-layouts, step(): jnp.zeros((row_blocks, CB, width), jnp.float32).at[local]  39.3 us
    reduce_scatter x1, waiting for transfers between devices, body(): lax.psum_scatter(result.reshape(row_count, total_blocks * CB), 'cam', sca...  38.2 us
    dot_general x16, matrix products, step(): jnp.einsum('rp,kcp->rkc', placed.reshape(row_count, width), block_panel.a...  36.7 us
    reshape x16, local copies, waits for them, and re-layouts, form_panel(): return jnp.stack(pieces, axis=-2).reshape(block_panel.shape)  28.5 us
  transfers between devices with their start and end apart: 2, of which 2 were waited for; matrix products, arithmetic and copies ran while one was open for 1% of the time, Pallas kernels for 0%

commit v1 on v0

v1 whole, which is shorter than its diff:
```python
import functools
import math

import jax
import jax.numpy as jnp
from jax import lax
from jax.experimental import pallas as pl
from jax.experimental.pallas import tpu as pltpu
from jax.sharding import PartitionSpec as P

CB = 64
LMB = 128
K = 16
WIDTH = 3 * LMB
STRIP = 16
VMEM = pl.BlockSpec(memory_space=pltpu.VMEM)
SMEM = pl.BlockSpec(memory_space=pltpu.SMEM)
PARAMS = pltpu.CompilerParams(vmem_limit_bytes=56 * 1024 * 1024)


def invert_rows(cur_ref, tile):
    lanes = slice(tile * LMB, (tile + 1) * LMB)
    entry = [[cur_ref[row, col : col + 1, lanes] for col in range(3)] for row in range(3)]
    cofactor = [
        [
            entry[(row + 1) % 3][(col + 1) % 3] * entry[(row + 2) % 3][(col + 2) % 3]
            - entry[(row + 1) % 3][(col + 2) % 3] * entry[(row + 2) % 3][(col + 1) % 3]
            for col in range(3)
        ]
        for row in range(3)
    ]
    determ = (
        entry[0][0] * cofactor[0][0] + entry[0][1] * cofactor[0][1] + entry[0][2] * cofactor[0][2]
    )
    return [[cofactor[col][row] / determ for col in range(3)] for row in range(3)]


def encode(dst, values, blocks):
    columns = values.shape[1]
    row = lax.broadcasted_iota(jnp.int32, (STRIP, columns), 0)
    strip = jnp.zeros((STRIP, columns), jnp.float32)
    for block in range(blocks):
        part = values[block * CB : (block + 1) * CB]
        top = jnp.max(jnp.abs(part), axis=0, keepdims=True)
        power = jnp.ceil(jnp.log2(jnp.maximum(top, 2.0**-100)) - 14.99)
        dst[pl.ds(block * CB, CB), :] = (
            jnp.round(part * jnp.exp2(-power)).astype(jnp.int32).astype(jnp.int16)
        )
        strip = jnp.where(row == block, power, strip)
    dst[pl.ds(blocks * CB, STRIP), :] = strip.astype(jnp.int32).astype(jnp.int16)


def decode(src, blocks):
    strip = src[pl.ds(blocks * CB, STRIP), :].astype(jnp.int32).astype(jnp.float32)
    scale = jnp.exp2(strip)
    return [
        src[pl.ds(block * CB, CB), :].astype(jnp.int32).astype(jnp.float32)
        * scale[block : block + 1]
        for block in range(blocks)
    ]


def partial_kernel(plan, me_ref, ids_a, ids_b, pan_a, pan_b, cur_a, cur_b, *rest):
    pieces, n_cam, row_blocks, chips, orders, tiles = plan
    sends, keeps = rest[:pieces], rest[pieces : 2 * pieces]
    cols, rows, acc, row_live, col_live = rest[2 * pieces :]
    piece, half, kind = pl.program_id(0), pl.program_id(1), pl.program_id(2)
    chip, core, cam = me_ref[0], me_ref[1], me_ref[2]
    group = acc.shape[1] // n_cam
    per = group // CB

    @pl.when((piece == 0) & (half == 0) & (kind == 0))
    def prepare():
        cols[...] = jnp.zeros_like(cols)
        rows[...] = jnp.zeros_like(rows)
        for tile in range(2 * tiles):
            for spot in range(chips):
                row_live[tile, spot] = 0
            for spot in range(pieces * n_cam):
                col_live[tile, spot] = 0
        for tile in range(2 * tiles):
            ids, pan, cur = (ids_a, pan_a, cur_a) if tile < tiles else (ids_b, pan_b, cur_b)
            here = tile % tiles
            inverse = invert_rows(cur, here)

            def place(slot, carry):
                ident = ids[here, slot]

                @pl.when(ident >= 0)
                def live():
                    panel = pan[here, slot]
                    inner = ident % (per * pieces)
                    column = (inner // per) * n_cam + ((ident // (per * pieces)) ^ cam)
                    start = pl.multiple_of((column * per + inner % per) * CB, CB)
                    cols[tile, pl.ds(start, CB), :] = panel
                    col_live[tile, column] = 1
                    owner = ident // row_blocks

                    @pl.when(owner % 2 == core)
                    def mine():
                        spot = (owner // 2) ^ chip
                        row_live[tile, spot] = 1
                        first = pl.multiple_of((spot * row_blocks + ident % row_blocks) * CB, CB)
                        wide = panel.astype(jnp.float32)
                        split = [wide[:, c * LMB : (c + 1) * LMB] for c in range(3)]
                        for target in range(3):
                            formed = (
                                split[0] * inverse[0][target]
                                + split[1] * inverse[1][target]
                                + split[2] * inverse[2][target]
                            )
                            high = formed.astype(jnp.bfloat16)
                            low = (formed - high.astype(jnp.float32)).astype(jnp.bfloat16)
                            lanes = slice(target * LMB, (target + 1) * LMB)
                            rows[tile, 0, pl.ds(first, CB), lanes] = high
                            rows[tile, 1, pl.ds(first, CB), lanes] = low

                return carry

            lax.fori_loop(0, K, place, 0)

    index = half + (1 - kind) * (chips // 2)
    bits = int(math.log2(chips))
    spot = jnp.int32(0)
    for which in range(pieces):
        value = jnp.int32(0)
        for place_of, bit in enumerate(orders[which]):
            value = value + (((index >> (bits - 1 - place_of)) & 1) << bit)
        spot = jnp.where(piece == which, value, spot)
    extent = row_blocks * CB
    first = pl.multiple_of(spot * extent, extent)
    acc[...] = jnp.zeros_like(acc)

    def columns_of(other, carry):
        column = piece * n_cam + other
        lanes = pl.ds(pl.multiple_of(other * group, group), group)
        start = pl.multiple_of(column * group, group)
        for tile in range(2 * tiles):

            @pl.when((row_live[tile, spot] > 0) & (col_live[tile, column] > 0))
            def add():
                right = cols[tile, pl.ds(start, group), :]
                total = acc[:, lanes]
                for level in range(2):
                    total = total + lax.dot_general(
                        rows[tile, level, pl.ds(first, extent), :],
                        right,
                        (((1,), (1,)), ((), ())),
                        preferred_element_type=jnp.float32,
                    )
                acc[:, lanes] = total

        return carry

    lax.fori_loop(0, n_cam, columns_of, 0)
    for which in range(pieces):

        @pl.when((piece == which) & (kind == 0))
        def send():
            encode(sends[which].at[0], acc[...], row_blocks)

        @pl.when((piece == which) & (kind == 1))
        def keep():
            keeps[which][0] = acc[...]


def relay_kernel(row_blocks, keep_ref, *rest):
    dst = rest[-1]
    total = keep_ref[0]
    for came in rest[:-1]:
        total = total + jnp.concatenate(decode(came.at[0], row_blocks), axis=0)
    encode(dst.at[0], total, row_blocks)


def finish_kernel(plan, me_ref, wide_ref, *rest):
    pieces, row_blocks, row_shift, col_blocks, counts = plan
    out_ref = rest[-1]
    cursor = 0
    group = out_ref.shape[1] // pieces
    first_row = (me_ref[0] * 2 + me_ref[1]) * row_blocks
    first_col = me_ref[2] * col_blocks
    for piece in range(pieces):
        keep = rest[cursor]
        came = rest[cursor + 1 : cursor + counts]
        cursor += counts
        parts = [decode(ref.at[0], row_blocks) for ref in came]
        for block in range(row_blocks):
            total = keep[0, pl.ds(block * CB, CB), :]
            for part in parts:
                total = total + part[block]
            for pair in range(group // (2 * CB)):
                lane = lax.broadcasted_iota(jnp.int32, (CB, 2 * CB), 1)
                base = first_col + (piece * group) // CB + 2 * pair
                hit = base + lane // CB == first_row + block
                wide = jnp.where(hit, wide_ref[block], 0.0)
                start = piece * group + pair * 2 * CB
                out_ref[pl.ds(block * CB, CB), pl.ds(start, 2 * CB)] = (
                    wide - total[:, pair * 2 * CB : (pair + 1) * 2 * CB]
                )


def body(panels, curvature, visible_blocks, counts, camera_hessian):
    tiles = panels.shape[0]
    n_lm, n_cam = lax.axis_size("lm"), lax.axis_size("cam")
    chips = n_lm // 2
    bits = int(math.log2(chips))
    row_blocks = camera_hessian.shape[0]
    extent = row_blocks * CB
    col_blocks = row_blocks * n_lm // n_cam
    pieces = 2
    group = col_blocks * CB // pieces
    columns = group * n_cam
    coded = extent + STRIP
    orders = [list(range(bits)), list(reversed(range(bits)))]
    lm, cam = lax.axis_index("lm"), lax.axis_index("cam")
    me = jnp.stack([lm // 2, lm % 2, cam]).astype(jnp.int32)

    live = jnp.arange(K, dtype=jnp.int32)[None, :] < counts[:, None]
    ids = jnp.where(live, visible_blocks, -1)

    def swap(value, bit):
        return lax.ppermute(value, "lm", [(i, i ^ (1 << bit)) for i in range(n_lm)])

    ids_other, cur_other, pan_other = swap(ids, 0), swap(curvature, 0), swap(panels, 0)

    def place_of(which):
        def index(piece, half, kind):
            inside = jnp.where(piece == which, half, jnp.where(piece < which, 0, chips // 2 - 1))
            return (inside, 0, 0)

        return index

    outs = pl.pallas_call(
        functools.partial(
            partial_kernel, (pieces, n_cam, row_blocks, chips, orders, tiles)
        ),
        grid=(pieces, chips // 2, 2),
        in_specs=[SMEM] * 3 + [VMEM] * 4,
        out_specs=[pl.BlockSpec((1, coded, columns), place_of(which)) for which in range(pieces)]
        + [pl.BlockSpec((1, extent, columns), place_of(which)) for which in range(pieces)],
        out_shape=[jax.ShapeDtypeStruct((chips // 2, coded, columns), jnp.int16)] * pieces
        + [jax.ShapeDtypeStruct((chips // 2, extent, columns), jnp.float32)] * pieces,
        scratch_shapes=[
            pltpu.VMEM((2 * tiles, pieces * columns, WIDTH), jnp.bfloat16),
            pltpu.VMEM((2 * tiles, 2, chips * extent, WIDTH), jnp.bfloat16),
            pltpu.VMEM((extent, columns), jnp.float32),
            pltpu.SMEM((2 * tiles, chips), jnp.int32),
            pltpu.SMEM((2 * tiles, pieces * n_cam), jnp.int32),
        ],
        compiler_params=PARAMS,
        name="partial",
    )(me, ids, ids_other, panels, pan_other, curvature, cur_other)
    sends, keeps = list(outs[:pieces]), outs[pieces:]

    came = [[] for _ in range(pieces)]
    for stage in range(bits):
        for piece in range(pieces):
            came[piece].append(swap(sends[piece], orders[piece][stage] + 1))
        size = chips >> (stage + 1)
        if size == 1:
            break
        for piece in range(pieces):
            arrays = [keeps[piece]] + came[piece]

            def later(half, block):
                return (size // 2 + half, 0, block)

            def out_at(half, block):
                return (half, 0, block)

            lanes = 256
            sends[piece] = pl.pallas_call(
                functools.partial(relay_kernel, row_blocks),
                grid=(size // 2, columns // lanes),
                in_specs=[pl.BlockSpec((1, extent, lanes), later)]
                + [pl.BlockSpec((1, coded, lanes), later)] * len(came[piece]),
                out_specs=pl.BlockSpec((1, coded, lanes), out_at),
                out_shape=jax.ShapeDtypeStruct((size // 2, coded, columns), jnp.int16),
                compiler_params=PARAMS,
                name="relay",
            )(*arrays)

    finals = []
    for piece in range(pieces):
        arrays = [keeps[piece]] + came[piece]

        def far(other):
            return (0, 0, other + 1)

        crossed = pl.pallas_call(
            functools.partial(relay_kernel, row_blocks),
            grid=(n_cam - 1,),
            in_specs=[pl.BlockSpec((1, extent, group), far)]
            + [pl.BlockSpec((1, coded, group), far)] * len(came[piece]),
            out_specs=pl.BlockSpec((1, coded, group), lambda other: (other, 0, 0)),
            out_shape=jax.ShapeDtypeStruct((n_cam - 1, coded, group), jnp.int16),
            compiler_params=PARAMS,
            name="cross",
        )(*arrays)
        last = [
            lax.ppermute(
                crossed[other - 1 : other], "cam", [(i, i ^ other) for i in range(n_cam)]
            )
            for other in range(1, n_cam)
        ]
        finals.append(arrays + last)

    wide = jnp.concatenate([camera_hessian, camera_hessian], axis=-1)
    specs, flat = [], []
    for piece in range(pieces):
        for pos, array in enumerate(finals[piece]):
            shape = (1, extent if pos == 0 else coded, group)
            specs.append(pl.BlockSpec(shape, lambda step: (0, 0, 0)))
            flat.append(array)
    return pl.pallas_call(
        functools.partial(
            finish_kernel, (pieces, row_blocks, chips, col_blocks, len(finals[0]))
        ),
        grid=(1,),
        in_specs=[SMEM, VMEM] + specs,
        out_specs=pl.BlockSpec((extent, col_blocks * CB), lambda step: (0, 0)),
        out_shape=jax.ShapeDtypeStruct((extent, col_blocks * CB), jnp.float32),
        compiler_params=PARAMS,
        name="finish",
    )(me, wide, *flat)


def solution(mesh):
    return jax.shard_map(
        body,
        mesh=mesh,
        in_specs=(
            P(("lm", "cam"), None, None, None),
            P(None, None, ("lm", "cam")),
            P(("lm", "cam"), None),
            P(("lm", "cam")),
            P("lm", None, None),
        ),
        out_specs=P("lm", "cam"),
        check_vma=False,
    )
```

time: 453 us -> 110 us (0.24)
  local copies, waits for them, and re-layouts: 149 us -> 8.88 us
  other arithmetic: 135 us -> 2.09 us
  waiting for transfers between devices: 92.8 us -> 43.5 us
  matrix products: 36.7 us -> 0 us
  Pallas kernels: 0 us -> 30.2 us
  starting transfers between devices: 0.04 us -> 25.8 us
  blocking collectives: 20.6 us -> 0 us
  between operations: 13.6 us -> 0.08 us
    all_gather x1 -> x0, waiting for transfers between devices: 54.6 us -> none  [body(): piece_panels = lax.all_gather(masked, 'lm', axis=0, tiled=True)]
    ppermute x0 -> x13, waiting for transfers between devices: none -> 43.5 us  [the longest x7 30.7 us: swap(): return lax.ppermute(value, 'lm', [(i, i ^ 1 << bit) for i in range(n_lm)])]
    add x16 -> x0, other arithmetic: 41.9 us -> none  [form_panel(): split[..., 0, :] * inverse[0, target]]
    convert_element_type x16 -> x0, local copies, waits for them, and re-layouts: 39.9 us -> none  [form_panel(): block_panel.astype(jnp.float32).reshape(block_panel.shape[:-1] + (3, LMB))]
    convert_element_type x16 -> x0, other arithmetic: 39.4 us -> none  [form_panel(): block_panel.astype(jnp.float32).reshape(block_panel.shape[:-1] + (3, LMB))]
    scatter x16 -> x0, local copies, waits for them, and re-layouts: 39.3 us -> none  [step(): jnp.zeros((row_blocks, CB, width), jnp.float32).at[local]]
    reduce_scatter x1 -> x0, waiting for transfers between devices: 38.2 us -> none  [body(): lax.psum_scatter(result.reshape(row_count, total_blocks * CB), 'cam', sca...]
    dot_general x16 -> x0, matrix products: 36.7 us -> none  [step(): jnp.einsum('rp,kcp->rkc', placed.reshape(row_count, width), block_panel.a...]
  transfers between devices with their start and end apart: 2 -> 13, of which waited for: 2 -> 6; matrix products, arithmetic and copies ran while one was open for 1% -> 4% of each run, Pallas kernels for 0% -> 12%
where the time goes in v1:
time: 110 us; the launch traced here: 111 us
  waiting for transfers between devices  43.5 us (40%)
  Pallas kernels  30.2 us (27%)
  starting transfers between devices  25.8 us (23%)
  local copies, waits for them, and re-layouts  8.88 us (8%)
  other arithmetic  2.09 us (2%)
    ppermute x7, waiting for transfers between devices, swap(): return lax.ppermute(value, 'lm', [(i, i ^ 1 << bit) for i in range(n_lm)])  30.7 us
    ppermute x7, starting transfers between devices, swap(): return lax.ppermute(value, 'lm', [(i, i ^ 1 << bit) for i in range(n_lm)])  16.6 us
    pallas_call x1, Pallas kernels, body(): pl.pallas_call(functools.partial(partial_kernel, (pieces, n_cam, row_bloc...  14 us
    ppermute x6, waiting for transfers between devices, body(): lax.ppermute(crossed[other - 1:other], 'cam', [(i, i ^ other) for i in ra...  12.9 us
    ppermute x6, starting transfers between devices, body(): lax.ppermute(crossed[other - 1:other], 'cam', [(i, i ^ other) for i in ra...  9.26 us
    pallas_call x2, Pallas kernels, body(): pl.pallas_call(functools.partial(relay_kernel, row_blocks), grid=(size //...  7.08 us
    unnamed x30, local copies, waits for them, and re-layouts  6.75 us
    pallas_call x2, Pallas kernels, body(): pl.pallas_call(functools.partial(relay_kernel, row_blocks), grid=(n_cam -...  6.35 us
  transfers between devices with their start and end apart: 13, of which 6 were waited for; matrix products, arithmetic and copies ran while one was open for 4% of the time, Pallas kernels for 12%

profile of v1, /device:TPU:0, one launch (start us, length us, event | category | flops | bytes accessed | tf_op | source)
XLA Modules:
  0.0 110.6 jit_solution(4869120793950252109)
XLA Ops:
  0.0 0.5 collective-permute-start.1
  0.5 0.8 compare_select_fusion.ids_a
  1.2 0.0 copy-start.13
  1.2 0.1 collective-permute-start
  1.3 0.5 collective-permute-start.2
  1.7 0.6 pad_add_fusion.me_ref
  2.3 1.2 %collective-permute-done.ids_b = s32[2,16]{1,0:T(2,128)S(1)} collective-permute-done((s32[2,16]{1,0:T(2,128)S(1)}, s32[2,16]{1,0:T(2,128)S(1)}, u32[]{:S(2)}, u32[]{:S(2)}) %collective-permute-start) | collective-permute-done | bytes 160 | tf_op jit(solution)/shard_map/ppermute | solution.py:222
  3.5 0.0 copy-start.14
  3.5 0.2 collective-permute-done.2.cur_b
  3.7 0.0 copy-start.12
  3.7 0.0 collective-permute-done.1.pan_b
  3.7 0.0 copy-done.13
  3.7 0.3 copy-done.14
  4.1 0.3 copy-done.12
  4.3 0.0 copy-start.4
  4.3 1.2 %copy-done.4 = bf16[2,16,64,384]{3,2,1,0:T(8,128)(2,1)} copy-done((bf16[2,16,64,384]{3,2,1,0:T(8,128)(2,1)}, bf16[2,16,64,384]{3,2,1,0:T(8,128)(2,1)S(1)}, u32[]{:S(2)}) %copy-start.4) | copy-done | bytes 1572888
  5.5 14.0 %partial.1 = (s16[2,272,1024]{2,1,0:T(8,128)(2,1)}, s16[2,272,1024]{2,1,0:T(8,128)(2,1)}, f32[2,256,1024]{2,1,0:T(8,128)}, f32[2,256,1024]{2,1,0:T(8,128)}) custom-call(s32[3]{0:T(128)} %pad_add_fusion.me_ref, s32[2,16]{1,0:T(2,128)} %copy-done.13, s32[2,16]{1,0:T(2,128)} %copy-done.14, bf16[2,16,64,384]{3,2,1,0:T(8,128)(2,1)} %pan_a.1, ...), custom_call_target="tpu_custom_call" | custom-call | tf_op jit(solution)/shard_map/partial/pallas_call | solution.py:233
  19.5 10.1 %collective-permute-start.3 = (s16[2,272,1024]{2,1,0:T(8,128)(2,1)}, s16[2,272,1024]{2,1,0:T(8,128)(2,1)S(1)}, u32[]{:S(2)}, u32[]{:S(2)}) collective-permute-start(s16[2,272,1024]{2,1,0:T(8,128)(2,1)} %get-tuple-element.10), channel_id=1, source_target_pairs={{0,8},{4,12},{8,0},{12,4},{16,24},{20,28},{24,16},{28,20},{1,9},{5... | collective-permute-start | bytes 3342344 | tf_op jit(solution)/shard_map/ppermute | solution.py:222
  29.6 2.3 %collective-permute-start.8 = (s16[2,272,1024]{2,1,0:T(8,128)(2,1)}, s16[2,272,1024]{2,1,0:T(8,128)(2,1)S(1)}, u32[]{:S(2)}, u32[]{:S(2)}) collective-permute-start(s16[2,272,1024]{2,1,0:T(8,128)(2,1)} %get-tuple-element.12), channel_id=1, source_target_pairs={{0,16},{4,20},{8,24},{12,28},{16,0},{20,4},{24,8},{28,12},{1,17},{... | collective-permute-start | bytes 3342344 | tf_op jit(solution)/shard_map/ppermute | solution.py:222
  31.9 22.7 %collective-permute-done.3.rest_0_.rest_1_ = s16[2,272,1024]{2,1,0:T(8,128)(2,1)S(1)} collective-permute-done((s16[2,272,1024]{2,1,0:T(8,128)(2,1)}, s16[2,272,1024]{2,1,0:T(8,128)(2,1)S(1)}, u32[]{:S(2)}, u32[]{:S(2)}) %collective-permute-start.3) | collective-permute-done | bytes 1114144 | tf_op jit(solution)/shard_map/ppermute | solution.py:222
  54.5 0.0 copy-start
  54.5 1.1 copy-done
  55.6 3.5 %relay.2 = s16[1,272,1024]{2,1,0:T(8,128)(2,1)} custom-call(f32[2,256,1024]{2,1,0:T(8,128)} %get-tuple-element.9.keep_ref.rest_0_, s16[2,272,1024]{2,1,0:T(8,128)(2,1)} %copy-done), custom_call_target="tpu_custom_call" | custom-call | tf_op jit(solution)/shard_map/relay/pallas_call | solution.py:272
  59.1 2.1 %collective-permute-start.4 = (s16[1,272,1024]{2,1,0:T(8,128)(2,1)}, s16[1,272,1024]{2,1,0:T(8,128)(2,1)S(1)}, u32[]{:S(2)}, u32[]{:S(2)}) collective-permute-start(s16[1,272,1024]{2,1,0:T(8,128)(2,1)} %relay.2), channel_id=1, source_target_pairs={{0,16},{4,20},{8,24},{12,28},{16,0},{20,4},{24,8},{28,12},{1,17},{... | collective-permute-start | bytes 1671176 | tf_op jit(solution)/shard_map/ppermute | solution.py:222
  61.2 0.0 collective-permute-done.8.rest_0_.rest_7_
  61.2 0.0 copy-start.1
  61.2 1.0 copy-done.1
  62.3 3.6 %relay.3 = s16[1,272,1024]{2,1,0:T(8,128)(2,1)} custom-call(f32[2,256,1024]{2,1,0:T(8,128)} %get-tuple-element.11.keep_ref.rest_6_, s16[2,272,1024]{2,1,0:T(8,128)(2,1)} %copy-done.1), custom_call_target="tpu_custom_call" | custom-call | tf_op jit(solution)/shard_map/relay/pallas_call | solution.py:272
  65.8 1.2 %collective-permute-start.9 = (s16[1,272,1024]{2,1,0:T(8,128)(2,1)}, s16[1,272,1024]{2,1,0:T(8,128)(2,1)S(1)}, u32[]{:S(2)}, u32[]{:S(2)}) collective-permute-start(s16[1,272,1024]{2,1,0:T(8,128)(2,1)} %relay.3), channel_id=1, source_target_pairs={{0,8},{4,12},{8,0},{12,4},{16,24},{20,28},{24,16},{28,20},{1,9},{5... | collective-permute-start | bytes 1671176 | tf_op jit(solution)/shard_map/ppermute | solution.py:222
  67.0 6.6 %collective-permute-done.4.rest_1_.rest_2_ = s16[1,272,1024]{2,1,0:T(8,128)(2,1)S(1)} collective-permute-done((s16[1,272,1024]{2,1,0:T(8,128)(2,1)}, s16[1,272,1024]{2,1,0:T(8,128)(2,1)S(1)}, u32[]{:S(2)}, u32[]{:S(2)}) %collective-permute-start.4) | collective-permute-done | bytes 557088 | tf_op jit(solution)/shard_map/ppermute | solution.py:222
  73.5 0.0 copy-start.2
  73.5 0.8 copy-done.2
  74.3 3.2 %cross.2 = s16[3,272,256]{2,1,0:T(8,128)(2,1)} custom-call(f32[2,256,1024]{2,1,0:T(8,128)} %get-tuple-element.9.keep_ref.rest_0_, s16[2,272,1024]{2,1,0:T(8,128)(2,1)} %copy-done, s16[1,272,1024]{2,1,0:T(8,128)(2,1)} %copy-done.2), custom_call_target="tpu_custom_call" | custom-call | tf_op jit(solution)/shard_map/cross/pallas_call | solution.py:290
  77.5 1.1 fusion.1
  78.6 4.0 %collective-permute-start.7 = (s16[1,272,256]{2,1,0:T(8,128)(2,1)S(1)}, s16[1,272,256]{2,1,0:T(8,128)(2,1)S(1)}, u32[]{:S(2)}, u32[]{:S(2)}) collective-permute-start(s16[1,272,256]{2,1,0:T(8,128)(2,1)S(1)} %get-tuple-element.16), channel_id=1, source_target_pairs={{0,3},{1,2},{2,1},{3,0},{4,7},{5,6},{6,5},{7,4},{8,11},{9,10},{10,... | collective-permute-start | bytes 417800 | tf_op jit(solution)/shard_map/ppermute | solution.py:301
  82.6 0.6 collective-permute-start.6
  83.2 0.0 copy-start.11
  83.2 0.2 collective-permute-start.5
  83.4 0.0 collective-permute-done.9.rest_1_.rest_8_
  83.4 0.0 copy-start.3
  83.4 0.8 copy-done.3
  84.2 3.2 %cross.3 = s16[3,272,256]{2,1,0:T(8,128)(2,1)} custom-call(f32[2,256,1024]{2,1,0:T(8,128)} %get-tuple-element.11.keep_ref.rest_6_, s16[2,272,1024]{2,1,0:T(8,128)(2,1)} %copy-done.1, s16[1,272,1024]{2,1,0:T(8,128)(2,1)} %copy-done.3), custom_call_target="tpu_custom_call" | custom-call | tf_op jit(solution)/shard_map/cross/pallas_call | solution.py:290
  87.4 1.1 fusion
  88.5 3.6 %collective-permute-start.12 = (s16[1,272,256]{2,1,0:T(8,128)(2,1)S(1)}, s16[1,272,256]{2,1,0:T(8,128)(2,1)S(1)}, u32[]{:S(2)}, u32[]{:S(2)}) collective-permute-start(s16[1,272,256]{2,1,0:T(8,128)(2,1)S(1)} %get-tuple-element.13), channel_id=1, source_target_pairs={{0,3},{1,2},{2,1},{3,0},{4,7},{5,6},{6,5},{7,4},{8,11},{9,10},{10,... | collective-permute-start | bytes 417800 | tf_op jit(solution)/shard_map/ppermute | solution.py:301
  92.1 0.0 collective-permute-start.11
  92.1 0.0 collective-permute-done.7.rest_5_
  92.1 0.0 copy-start.5
  92.1 0.8 collective-permute-start.10
  92.9 0.0 copy-done.11
  92.9 0.8 pad_maximum_fusion.wide_ref
  93.7 6.9 %collective-permute-done.6.rest_4_ = s16[1,272,256]{2,1,0:T(8,128)(2,1)S(1)} collective-permute-done((s16[1,272,256]{2,1,0:T(8,128)(2,1)S(1)}, s16[1,272,256]{2,1,0:T(8,128)(2,1)S(1)}, u32[]{:S(2)}, u32[]{:S(2)}) %collective-permute-start.6) | collective-permute-done | bytes 139296 | tf_op jit(solution)/shard_map/ppermute | solution.py:301
  100.6 0.0 copy-start.6
  100.6 0.0 collective-permute-done.5.rest_3_
  100.6 0.0 collective-permute-done.12.rest_11_
  100.6 0.0 copy-start.8
  100.6 5.9 %collective-permute-done.11.rest_10_ = s16[1,272,256]{2,1,0:T(8,128)(2,1)S(1)} collective-permute-done((s16[1,272,256]{2,1,0:T(8,128)(2,1)S(1)}, s16[1,272,256]{2,1,0:T(8,128)(2,1)S(1)}, u32[]{:S(2)}, u32[]{:S(2)}) %collective-permute-start.11) | collective-permute-done | bytes 139296 | tf_op jit(solution)/shard_map/ppermute | solution.py:301
  106.6 0.0 collective-permute-done.10.rest_9_
  106.6 0.0 copy-done.5
  106.6 0.0 copy-done.6
  106.6 0.0 copy-done.7
  106.6 0.0 copy-done.8
  106.6 0.6 copy-done.9
  107.2 0.6 copy-done.10
  107.9 2.7 %finish.1 = f32[256,512]{1,0:T(8,128)} custom-call(s32[3]{0:T(128)} %pad_add_fusion.me_ref, f32[4,64,128]{2,1,0:T(8,128)} %pad_maximum_fusion.wide_ref, f32[2,256,1024]{2,1,0:T(8,128)} %get-tuple-element.9.keep_ref.rest_0_, s16[2,272,1024]{2,1,0:T(8,128)(2,1)} %copy-done, s16[1,272,1024]{2,1,0:T(8,128)(2,1)} %copy-done.2, s16[1,272,256]{2,1,0:T(8,128)(2,1)} %copy-done.7, ...), custom_call_target="tpu_custom_call" | custom-call | tf_op jit(solution)/shard_map/finish/pallas_call | solution.py:315
  (3 shorter events, 0.0 us)
Async XLA Ops:
  0.0 3.7 %collective-permute-start.1 = (bf16[2,16,64,384]{3,2,1,0:T(8,128)(2,1)}, bf16[2,16,64,384]{3,2,1,0:T(8,128)(2,1)S(1)}, u32[]{:S(2)}, u32[]{:S(2)}) collective-permute-start(bf16[2,16,64,384]{3,2,1,0:T(8,128)(2,1)} %pan_a.1), channel_id=1, source_target_pairs={{0,4},{4,0},{8,12},{12,8},{16,20},{20,16},{24,28},{28,24},{1,5},{5... | collective-permute-start | bytes 4718600 | tf_op jit(solution)/shard_map/ppermute | solution.py:222
  1.2 2.5 %copy-start.13 = (s32[2,16]{1,0:T(2,128)}, s32[2,16]{1,0:T(2,128)S(1)}, u32[]{:S(2)}) copy-start(s32[2,16]{1,0:T(2,128)S(1)} %compare_select_fusion.ids_a) | copy-start | bytes 388
  1.2 2.3 %collective-permute-start = (s32[2,16]{1,0:T(2,128)S(1)}, s32[2,16]{1,0:T(2,128)S(1)}, u32[]{:S(2)}, u32[]{:S(2)}) collective-permute-start(s32[2,16]{1,0:T(2,128)S(1)} %compare_select_fusion.ids_a), channel_id=1, source_target_pairs={{0,4},{4,0},{8,12},{12,8},{16,20},{20,16},{24,28},{28,24},{1,5},{5... | collective-permute-start | bytes 392 | tf_op jit(solution)/shard_map/ppermute | solution.py:222
  1.3 2.5 %collective-permute-start.2 = (f32[3,3,256]{2,1,0:T(4,128)}, f32[3,3,256]{2,1,0:T(4,128)S(1)}, u32[]{:S(2)}, u32[]{:S(2)}) collective-permute-start(f32[3,3,256]{2,1,0:T(4,128)} %cur_a.1), channel_id=1, source_target_pairs={{0,4},{4,0},{8,12},{12,8},{16,20},{20,16},{24,28},{28,24},{1,5},{5... | collective-permute-start | bytes 27656 | tf_op jit(solution)/shard_map/ppermute | solution.py:222
  3.5 0.6 copy-start.14
  3.7 0.6 copy-start.12
  4.3 1.2 %copy-start.4 = (bf16[2,16,64,384]{3,2,1,0:T(8,128)(2,1)}, bf16[2,16,64,384]{3,2,1,0:T(8,128)(2,1)S(1)}, u32[]{:S(2)}) copy-start(bf16[2,16,64,384]{3,2,1,0:T(8,128)(2,1)S(1)} %collective-permute-done.1.pan_b) | copy-start | bytes 4718596
  19.5 35.0 %collective-permute-start.3 = (s16[2,272,1024]{2,1,0:T(8,128)(2,1)}, s16[2,272,1024]{2,1,0:T(8,128)(2,1)S(1)}, u32[]{:S(2)}, u32[]{:S(2)}) collective-permute-start(s16[2,272,1024]{2,1,0:T(8,128)(2,1)} %get-tuple-element.10), channel_id=1, source_target_pairs={{0,8},{4,12},{8,0},{12,4},{16,24},{20,28},{24,16},{28,20},{1,9},{5... | collective-permute-start | bytes 3342344 | tf_op jit(solution)/shard_map/ppermute | solution.py:222
  29.6 31.6 %collective-permute-start.8 = (s16[2,272,1024]{2,1,0:T(8,128)(2,1)}, s16[2,272,1024]{2,1,0:T(8,128)(2,1)S(1)}, u32[]{:S(2)}, u32[]{:S(2)}) collective-permute-start(s16[2,272,1024]{2,1,0:T(8,128)(2,1)} %get-tuple-element.12), channel_id=1, source_target_pairs={{0,16},{4,20},{8,24},{12,28},{16,0},{20,4},{24,8},{28,12},{1,17},{... | collective-permute-start | bytes 3342344 | tf_op jit(solution)/shard_map/ppermute | solution.py:222
  54.5 1.1 copy-start
  59.1 14.4 %collective-permute-start.4 = (s16[1,272,1024]{2,1,0:T(8,128)(2,1)}, s16[1,272,1024]{2,1,0:T(8,128)(2,1)S(1)}, u32[]{:S(2)}, u32[]{:S(2)}) collective-permute-start(s16[1,272,1024]{2,1,0:T(8,128)(2,1)} %relay.2), channel_id=1, source_target_pairs={{0,16},{4,20},{8,24},{12,28},{16,0},{20,4},{24,8},{28,12},{1,17},{... | collective-permute-start | bytes 1671176 | tf_op jit(solution)/shard_map/ppermute | solution.py:222
  61.2 1.0 copy-start.1
  65.8 17.6 %collective-permute-start.9 = (s16[1,272,1024]{2,1,0:T(8,128)(2,1)}, s16[1,272,1024]{2,1,0:T(8,128)(2,1)S(1)}, u32[]{:S(2)}, u32[]{:S(2)}) collective-permute-start(s16[1,272,1024]{2,1,0:T(8,128)(2,1)} %relay.3), channel_id=1, source_target_pairs={{0,8},{4,12},{8,0},{12,4},{16,24},{20,28},{24,16},{28,20},{1,9},{5... | collective-permute-start | bytes 1671176 | tf_op jit(solution)/shard_map/ppermute | solution.py:222
  73.5 0.8 copy-start.2
  78.6 13.5 %collective-permute-start.7 = (s16[1,272,256]{2,1,0:T(8,128)(2,1)S(1)}, s16[1,272,256]{2,1,0:T(8,128)(2,1)S(1)}, u32[]{:S(2)}, u32[]{:S(2)}) collective-permute-start(s16[1,272,256]{2,1,0:T(8,128)(2,1)S(1)} %get-tuple-element.16), channel_id=1, source_target_pairs={{0,3},{1,2},{2,1},{3,0},{4,7},{5,6},{6,5},{7,4},{8,11},{9,10},{10,... | collective-permute-start | bytes 417800 | tf_op jit(solution)/shard_map/ppermute | solution.py:301
  82.6 18.0 %collective-permute-start.6 = (s16[1,272,256]{2,1,0:T(8,128)(2,1)S(1)}, s16[1,272,256]{2,1,0:T(8,128)(2,1)S(1)}, u32[]{:S(2)}, u32[]{:S(2)}) collective-permute-start(s16[1,272,256]{2,1,0:T(8,128)(2,1)S(1)} %get-tuple-element.17), channel_id=1, source_target_pairs={{0,2},{1,3},{2,0},{3,1},{4,6},{5,7},{6,4},{7,5},{8,10},{9,11},{10,... | collective-permute-start | bytes 417800 | tf_op jit(solution)/shard_map/ppermute | solution.py:301
  83.2 9.8 %copy-start.11 = (f32[4,64,64]{2,1,0:T(8,128)S(1)}, f32[4,64,64]{2,1,0:T(8,128)}, u32[]{:S(2)}) copy-start(f32[4,64,64]{2,1,0:T(8,128)} %param.9) | copy-start | bytes 196612
  83.2 17.4 %collective-permute-start.5 = (s16[1,272,256]{2,1,0:T(8,128)(2,1)S(1)}, s16[1,272,256]{2,1,0:T(8,128)(2,1)S(1)}, u32[]{:S(2)}, u32[]{:S(2)}) collective-permute-start(s16[1,272,256]{2,1,0:T(8,128)(2,1)S(1)} %get-tuple-element.18), channel_id=1, source_target_pairs={{0,1},{1,0},{2,3},{3,2},{4,5},{5,4},{6,7},{7,6},{8,9},{9,8},{10,11... | collective-permute-start | bytes 417800 | tf_op jit(solution)/shard_map/ppermute | solution.py:301
  83.4 0.8 copy-start.3
  88.5 12.1 %collective-permute-start.12 = (s16[1,272,256]{2,1,0:T(8,128)(2,1)S(1)}, s16[1,272,256]{2,1,0:T(8,128)(2,1)S(1)}, u32[]{:S(2)}, u32[]{:S(2)}) collective-permute-start(s16[1,272,256]{2,1,0:T(8,128)(2,1)S(1)} %get-tuple-element.13), channel_id=1, source_target_pairs={{0,3},{1,2},{2,1},{3,0},{4,7},{5,6},{6,5},{7,4},{8,11},{9,10},{10,... | collective-permute-start | bytes 417800 | tf_op jit(solution)/shard_map/ppermute | solution.py:301
  92.1 14.4 %collective-permute-start.11 = (s16[1,272,256]{2,1,0:T(8,128)(2,1)S(1)}, s16[1,272,256]{2,1,0:T(8,128)(2,1)S(1)}, u32[]{:S(2)}, u32[]{:S(2)}) collective-permute-start(s16[1,272,256]{2,1,0:T(8,128)(2,1)S(1)} %get-tuple-element.14), channel_id=1, source_target_pairs={{0,2},{1,3},{2,0},{3,1},{4,6},{5,7},{6,4},{7,5},{8,10},{9,11},{10,... | collective-permute-start | bytes 417800 | tf_op jit(solution)/shard_map/ppermute | solution.py:301
  92.1 14.4 %copy-start.5 = (s16[1,272,256]{2,1,0:T(8,128)(2,1)}, s16[1,272,256]{2,1,0:T(8,128)(2,1)S(1)}, u32[]{:S(2)}) copy-start(s16[1,272,256]{2,1,0:T(8,128)(2,1)S(1)} %collective-permute-done.7.rest_5_) | copy-start | bytes 417796
  92.1 14.4 %collective-permute-start.10 = (s16[1,272,256]{2,1,0:T(8,128)(2,1)S(1)}, s16[1,272,256]{2,1,0:T(8,128)(2,1)S(1)}, u32[]{:S(2)}, u32[]{:S(2)}) collective-permute-start(s16[1,272,256]{2,1,0:T(8,128)(2,1)S(1)} %get-tuple-element.15), channel_id=1, source_target_pairs={{0,1},{1,0},{2,3},{3,2},{4,5},{5,4},{6,7},{7,6},{8,9},{9,8},{10,11... | collective-permute-start | bytes 417800 | tf_op jit(solution)/shard_map/ppermute | solution.py:301
  100.6 6.0 %copy-start.6 = (s16[1,272,256]{2,1,0:T(8,128)(2,1)}, s16[1,272,256]{2,1,0:T(8,128)(2,1)S(1)}, u32[]{:S(2)}) copy-start(s16[1,272,256]{2,1,0:T(8,128)(2,1)S(1)} %collective-permute-done.6.rest_4_) | copy-start | bytes 417796
  100.6 6.0 %copy-start.7 = (s16[1,272,256]{2,1,0:T(8,128)(2,1)}, s16[1,272,256]{2,1,0:T(8,128)(2,1)S(1)}, u32[]{:S(2)}) copy-start(s16[1,272,256]{2,1,0:T(8,128)(2,1)S(1)} %collective-permute-done.5.rest_3_) | copy-start | bytes 417796
  100.6 6.0 %copy-start.8 = (s16[1,272,256]{2,1,0:T(8,128)(2,1)}, s16[1,272,256]{2,1,0:T(8,128)(2,1)S(1)}, u32[]{:S(2)}) copy-start(s16[1,272,256]{2,1,0:T(8,128)(2,1)S(1)} %collective-permute-done.12.rest_11_) | copy-start | bytes 417796
  106.6 0.7 copy-start.9
  107.2 0.6 copy-start.10

commit v2 on v0

v2 whole, which is shorter than its diff:
```python
import functools
import math

import jax
import jax.numpy as jnp
from jax import lax
from jax.experimental import pallas as pl
from jax.experimental.pallas import tpu as pltpu
from jax.sharding import PartitionSpec as P

CB = 64
LMB = 128
K = 16
WIDTH = 3 * LMB
STRIP = 16
LANES = 128
CHUNK = 256
QUAD = CHUNK // CB
VMEM = pl.BlockSpec(memory_space=pltpu.VMEM)
SMEM = pl.BlockSpec(memory_space=pltpu.SMEM)
PARAMS = pltpu.CompilerParams(vmem_limit_bytes=32 * 1024 * 1024)


def invert_rows(cur_ref, tile):
    lanes = slice(tile * LMB, (tile + 1) * LMB)
    entry = [[cur_ref[row, col : col + 1, lanes] for col in range(3)] for row in range(3)]
    cofactor = [
        [
            entry[(row + 1) % 3][(col + 1) % 3] * entry[(row + 2) % 3][(col + 2) % 3]
            - entry[(row + 1) % 3][(col + 2) % 3] * entry[(row + 2) % 3][(col + 1) % 3]
            for col in range(3)
        ]
        for row in range(3)
    ]
    determ = (
        entry[0][0] * cofactor[0][0] + entry[0][1] * cofactor[0][1] + entry[0][2] * cofactor[0][2]
    )
    return [[cofactor[col][row] / determ for col in range(3)] for row in range(3)]


def encode(dst, lanes, parts):
    blocks = len(parts)
    row = lax.broadcasted_iota(jnp.int32, (8, LANES), 0)
    tops = jnp.full((8, LANES), 2.0**-100, jnp.float32)
    for block, part in enumerate(parts):
        top = jnp.max(jnp.abs(part), axis=0, keepdims=True)
        tops = jnp.where(row == block, jnp.maximum(top, tops), tops)
    power = jnp.ceil(jnp.log2(tops) - 14.99)
    inverse = jnp.exp2(-power)
    for block, part in enumerate(parts):
        coded = jnp.round(part * inverse[block : block + 1])
        dst[pl.ds(block * CB, CB), lanes] = coded.astype(jnp.int32).astype(jnp.int16)
    strip = jnp.concatenate([power, power], axis=0).astype(jnp.int32)
    dst[pl.ds(blocks * CB, STRIP), lanes] = strip.astype(jnp.int16)


def decode(src, lanes, blocks):
    strip = src[pl.ds(blocks * CB, STRIP), lanes].astype(jnp.int32).astype(jnp.float32)
    scale = jnp.exp2(strip)
    return [
        src[pl.ds(block * CB, CB), lanes].astype(jnp.int32).astype(jnp.float32)
        * scale[block : block + 1]
        for block in range(blocks)
    ]


def gathered(keep, came, lanes, blocks):
    parts = [keep[pl.ds(block * CB, CB), lanes] for block in range(blocks)]
    for src in came:
        parts = [part + other for part, other in zip(parts, decode(src, lanes, blocks))]
    return parts


def spot_of(index, order):
    bits = len(order)
    return sum(((index >> (bits - 1 - pos)) & 1) << bit for pos, bit in enumerate(order))


def partial_kernel(plan, me_ref, ids_a, ids_b, pan_a, pan_b, cur_a, cur_b, *rest):
    turn, per, pieces, n_cam, row_blocks, chips, orders, tiles, chunks = plan
    sends, keeps = rest[:2], rest[2:4]
    rows, right, acc, slot_at, row_at, many, busy = rest[4:]
    step = pl.program_id(0)
    chip, core, cam = me_ref[0], me_ref[1], me_ref[2]
    extent = row_blocks * CB
    total_chunks = 2 * chunks

    @pl.when(step == 0)
    def prepare():
        def clear(spot, carry):
            for tile in range(2 * tiles):
                slot_at[tile, spot] = -1
            return carry

        lax.fori_loop(0, total_chunks * QUAD, clear, 0)
        for tile in range(2 * tiles):
            for chunk in range(total_chunks):
                busy[tile, chunk] = 0
        for tile in range(2 * tiles):
            ids, pan, cur = (ids_a, pan_a, cur_a) if tile < tiles else (ids_b, pan_b, cur_b)
            here = tile % tiles
            inverse = invert_rows(cur, here)

            def place(slot, count):
                ident = ids[here, slot]
                live = ident >= 0
                known = jnp.maximum(ident, 0)
                inner = known % (per * pieces)
                piece = inner // per - 2 * turn
                column = piece * n_cam + ((known // (per * pieces)) ^ cam)
                spot = column * per + inner % per

                @pl.when(live & (piece >= 0) & (piece < 2))
                def listed():
                    slot_at[tile, spot] = slot
                    busy[tile, spot // QUAD] = 1

                owner = known // row_blocks
                mine = live & (owner % 2 == core)

                @pl.when(mine)
                def form():
                    group = (owner // 2) ^ chip
                    row_at[tile, count] = (group * row_blocks + known % row_blocks) * CB
                    first = pl.multiple_of(count * CB, CB)
                    wide = pan[here, slot].astype(jnp.float32)
                    split = [wide[:, c * LMB : (c + 1) * LMB] for c in range(3)]
                    for target in range(3):
                        formed = (
                            split[0] * inverse[0][target]
                            + split[1] * inverse[1][target]
                            + split[2] * inverse[2][target]
                        )
                        high = formed.astype(jnp.bfloat16)
                        low = (formed - high.astype(jnp.float32)).astype(jnp.bfloat16)
                        at = target * LMB
                        rows[tile, pl.ds(first, CB), at : at + LMB] = high
                        rows[tile, pl.ds(first, CB), WIDTH + at : WIDTH + at + LMB] = low

                return count + jnp.where(mine, 1, 0)

            count = lax.fori_loop(0, K, place, jnp.int32(0))
            many[tile] = (count + QUAD - 1) // QUAD
            for extra in range(QUAD):
                row_at[tile, count + extra] = chips * extent

    acc[...] = jnp.zeros_like(acc)
    for tile in range(2 * tiles):
        pan, here = (pan_a if tile < tiles else pan_b), tile % tiles

        @pl.when(busy[tile, step] > 0)
        def add():
            for quarter in range(QUAD):
                slot = slot_at[tile, step * QUAD + quarter]
                lines = slice(quarter * CB, (quarter + 1) * CB)

                @pl.when(slot >= 0)
                def fill():
                    panel = pan[here, slot]
                    right[tile % 2, lines, :WIDTH] = panel
                    right[tile % 2, lines, WIDTH:] = panel

                @pl.when(slot < 0)
                def blank():
                    right[tile % 2, lines, :] = jnp.zeros((CB, 2 * WIDTH), jnp.bfloat16)

            def product(group, carry):
                first = pl.multiple_of(group * QUAD * CB, QUAD * CB)
                result = lax.dot_general(
                    rows[tile, pl.ds(first, QUAD * CB), :],
                    right[tile % 2],
                    (((1,), (1,)), ((), ())),
                    preferred_element_type=jnp.float32,
                )
                for quarter in range(QUAD):
                    at = pl.multiple_of(row_at[tile, group * QUAD + quarter], CB)
                    acc[pl.ds(at, CB), :] += result[quarter * CB : (quarter + 1) * CB]
                return carry

            lax.fori_loop(0, many[tile], product, 0)

    for which in range(2):

        @pl.when(step // chunks == which)
        def store():
            for half in range(chips // 2):
                first = spot_of(half + chips // 2, orders[which]) * extent
                for start in range(0, CHUNK, LANES):
                    lanes = pl.ds(start, LANES)
                    parts = [
                        acc[pl.ds(first + block * CB, CB), lanes] for block in range(row_blocks)
                    ]
                    encode(sends[which].at[half], lanes, parts)
                first = spot_of(half, orders[which]) * extent
                keeps[which][half] = acc[pl.ds(first, extent), :]


def relay_kernel(row_blocks, keep_ref, *rest):
    dst = rest[-1].at[0]
    for start in range(0, dst.shape[1], LANES):
        lanes = pl.ds(start, LANES)
        came = [ref.at[0] for ref in rest[:-1]]
        encode(dst, lanes, gathered(keep_ref.at[0], came, lanes, row_blocks))


def cross_kernel(row_blocks, group, arrays, *rest):
    dsts = rest[2 * arrays :]
    for piece in range(2):
        keep = rest[piece * arrays].at[0]
        came = [ref.at[0] for ref in rest[piece * arrays + 1 : (piece + 1) * arrays]]
        for other, dst in enumerate(dsts):
            for start in range(0, group, LANES):
                lanes = pl.ds((other + 1) * group + start, LANES)
                parts = gathered(keep, came, lanes, row_blocks)
                encode(dst.at[piece], pl.ds(start, LANES), parts)


def finish_kernel(plan, me_ref, wide_ref, *rest):
    turn, row_blocks, col_blocks, arrays, far = plan
    out_ref = rest[-1]
    group = out_ref.shape[1] // 2
    first_row = (me_ref[0] * 2 + me_ref[1]) * row_blocks
    first_col = me_ref[2] * col_blocks
    lane = lax.broadcasted_iota(jnp.int32, (CB, LANES), 1) // CB
    for piece in range(2):
        keep = rest[piece * arrays].at[0]
        came = [ref.at[0] for ref in rest[piece * arrays + 1 : (piece + 1) * arrays]]
        came += [ref.at[piece] for ref in rest[2 * arrays : 2 * arrays + far]]
        for start in range(0, group, LANES):
            parts = gathered(keep, came, pl.ds(start, LANES), row_blocks)
            base = first_col + ((2 * turn + piece) * group + start) // CB
            for block in range(row_blocks):
                wide = jnp.where(base + lane == first_row + block, wide_ref[block], 0.0)
                out_ref[pl.ds(block * CB, CB), pl.ds(piece * group + start, LANES)] = (
                    wide - parts[block]
                )


def body(panels, curvature, visible_blocks, counts, camera_hessian):
    tiles = panels.shape[0]
    n_lm, n_cam = lax.axis_size("lm"), lax.axis_size("cam")
    chips = n_lm // 2
    bits = int(math.log2(chips))
    row_blocks = camera_hessian.shape[0]
    extent = row_blocks * CB
    col_blocks = row_blocks * n_lm // n_cam
    turns = col_blocks * CB // (2 * LANES)
    pieces = 2 * turns
    group = col_blocks * CB // pieces
    columns = group * n_cam
    chunks = columns // CHUNK
    coded = extent + STRIP
    orders = [list(range(bits)), list(reversed(range(bits)))]
    lm, cam = lax.axis_index("lm"), lax.axis_index("cam")
    me = jnp.stack([lm // 2, lm % 2, cam]).astype(jnp.int32)

    live = jnp.arange(K, dtype=jnp.int32)[None, :] < counts[:, None]
    ids = jnp.where(live, visible_blocks, -1)

    def swap(value, bit):
        return lax.ppermute(value, "lm", [(i, i ^ (1 << bit)) for i in range(n_lm)])

    ids_other, cur_other, pan_other = swap(ids, 0), swap(curvature, 0), swap(panels, 0)
    wide = jnp.concatenate([camera_hessian, camera_hessian], axis=-1)

    def piece_block(which):
        return lambda step: (0, 0, jnp.clip(step - which * chunks, 0, chunks - 1))

    sends, keeps = [], []
    for turn in range(turns):
        outs = pl.pallas_call(
            functools.partial(
                partial_kernel,
                (
                    turn,
                    group // CB,
                    pieces,
                    n_cam,
                    row_blocks,
                    chips,
                    orders,
                    tiles,
                    chunks,
                ),
            ),
            grid=(2 * chunks,),
            in_specs=[SMEM] * 3 + [VMEM] * 4,
            out_specs=[pl.BlockSpec((chips // 2, coded, CHUNK), piece_block(w)) for w in range(2)]
            + [pl.BlockSpec((chips // 2, extent, CHUNK), piece_block(w)) for w in range(2)],
            out_shape=[jax.ShapeDtypeStruct((chips // 2, coded, columns), jnp.int16)] * 2
            + [jax.ShapeDtypeStruct((chips // 2, extent, columns), jnp.float32)] * 2,
            scratch_shapes=[
                pltpu.VMEM((2 * tiles, K * CB, 2 * WIDTH), jnp.bfloat16),
                pltpu.VMEM((2, CHUNK, 2 * WIDTH), jnp.bfloat16),
                pltpu.VMEM((chips * extent + CB, CHUNK), jnp.float32),
                pltpu.SMEM((2 * tiles, 2 * chunks * QUAD), jnp.int32),
                pltpu.SMEM((2 * tiles, K + QUAD), jnp.int32),
                pltpu.SMEM((2 * tiles,), jnp.int32),
                pltpu.SMEM((2 * tiles, 2 * chunks), jnp.int32),
            ],
            compiler_params=PARAMS,
            name="partial",
        )(me, ids, ids_other, panels, pan_other, curvature, cur_other)
        sends.append(list(outs[:2]))
        keeps.append(outs[2:])

    came = [[[], []] for _ in range(turns)]
    result = None
    for turn in range(turns):
        for stage in range(bits):
            for piece in range(2):
                came[turn][piece].append(swap(sends[turn][piece], orders[piece][stage] + 1))
            size = chips >> (stage + 1)
            if size == 1:
                break
            for piece in range(2):
                arrays = [keeps[turn][piece]] + came[turn][piece]

                def later(half, block, size=size):
                    return (size // 2 + half, 0, block)

                sends[turn][piece] = pl.pallas_call(
                    functools.partial(relay_kernel, row_blocks),
                    grid=(size // 2, columns // CHUNK),
                    in_specs=[pl.BlockSpec((1, extent, CHUNK), later)]
                    + [pl.BlockSpec((1, coded, CHUNK), later)] * (len(arrays) - 1),
                    out_specs=pl.BlockSpec((1, coded, CHUNK), lambda half, block: (half, 0, block)),
                    out_shape=jax.ShapeDtypeStruct((size // 2, coded, columns), jnp.int16),
                    compiler_params=PARAMS,
                    name="relay",
                )(*arrays)

        near = [array for piece in range(2) for array in [keeps[turn][piece]] + came[turn][piece]]
        arrays = len(near) // 2

        def first(width):
            return [
                pl.BlockSpec((1, coded if pos % arrays else extent, width), lambda step: (0, 0, 0))
                for pos in range(2 * arrays)
            ]

        crossed = pl.pallas_call(
            functools.partial(cross_kernel, row_blocks, group, arrays),
            grid=(1,),
            in_specs=first(columns),
            out_specs=[pl.BlockSpec((2, coded, group), lambda step: (0, 0, 0))] * (n_cam - 1),
            out_shape=[jax.ShapeDtypeStruct((2, coded, group), jnp.int16)] * (n_cam - 1),
            compiler_params=PARAMS,
            name="cross",
        )(*near)
        far = [
            lax.ppermute(value, "cam", [(i, i ^ (pos + 1)) for i in range(n_cam)])
            for pos, value in enumerate(crossed)
        ]
        before = [] if result is None else [result]
        result = pl.pallas_call(
            functools.partial(finish_kernel, (turn, row_blocks, col_blocks, arrays, n_cam - 1)),
            grid=(1,),
            in_specs=[SMEM, VMEM]
            + first(group)
            + [pl.BlockSpec((2, coded, group), lambda step: (0, 0, 0))] * (n_cam - 1)
            + [pl.BlockSpec(memory_space=pl.ANY)] * len(before),
            out_specs=pl.BlockSpec((extent, 2 * group), lambda step, turn=turn: (0, turn)),
            out_shape=jax.ShapeDtypeStruct((extent, col_blocks * CB), jnp.float32),
            input_output_aliases={2 + len(near) + len(far): 0} if before else {},
            compiler_params=PARAMS,
            name="finish",
        )(me, wide, *near, *far, *before)
    return result


def solution(mesh):
    return jax.shard_map(
        body,
        mesh=mesh,
        in_specs=(
            P(("lm", "cam"), None, None, None),
            P(None, None, ("lm", "cam")),
            P(("lm", "cam"), None),
            P(("lm", "cam")),
            P("lm", None, None),
        ),
        out_specs=P("lm", "cam"),
        check_vma=False,
    )
```

time: 453 us -> 86.1 us (0.19); the launches traced: 449 us -> 86.7 us
  local copies, waits for them, and re-layouts: 149 us -> 2.12 us
  other arithmetic: 135 us -> 0.92 us
  waiting for transfers between devices: 92.8 us -> 33.1 us
  matrix products: 36.7 us -> 0 us
  Pallas kernels: 0 us -> 26.9 us
  starting transfers between devices: 0.04 us -> 23.5 us
  blocking collectives: 20.6 us -> 0 us
  between operations: 13.6 us -> 0.11 us
    all_gather x1 -> x0, waiting for transfers between devices: 54.6 us -> none  [body(): piece_panels = lax.all_gather(masked, 'lm', axis=0, tiled=True)]
    add x16 -> x0, other arithmetic: 41.9 us -> none  [form_panel(): split[..., 0, :] * inverse[0, target]]
    convert_element_type x16 -> x0, local copies, waits for them, and re-layouts: 39.9 us -> none  [form_panel(): block_panel.astype(jnp.float32).reshape(block_panel.shape[:-1] + (3, LMB))]
    convert_element_type x16 -> x0, other arithmetic: 39.4 us -> none  [form_panel(): block_panel.astype(jnp.float32).reshape(block_panel.shape[:-1] + (3, LMB))]
    scatter x16 -> x0, local copies, waits for them, and re-layouts: 39.3 us -> none  [step(): jnp.zeros((row_blocks, CB, width), jnp.float32).at[local]]
    reduce_scatter x1 -> x0, waiting for transfers between devices: 38.2 us -> none  [body(): lax.psum_scatter(result.reshape(row_count, total_blocks * CB), 'cam', sca...]
    dot_general x16 -> x0, matrix products: 36.7 us -> none  [step(): jnp.einsum('rp,kcp->rkc', placed.reshape(row_count, width), block_panel.a...]
    ppermute x0 -> x17, waiting for transfers between devices: none -> 33.1 us  [the longest x11 19.3 us: swap(): return lax.ppermute(value, 'lm', [(i, i ^ 1 << bit) for i in range(n_lm)])]
  transfers between devices with their start and end apart: 2 -> 17, of which waited for: 2 -> 7; matrix products, arithmetic and copies ran while one was open for 1% -> 1% of each run, Pallas kernels for 0% -> 18%
where the time goes in v2:
time: 86.1 us; the launch traced here: 86.7 us
  waiting for transfers between devices  33.1 us (38%)
  Pallas kernels  26.9 us (31%)
  starting transfers between devices  23.5 us (27%)
  local copies, waits for them, and re-layouts  2.12 us (2%)
  other arithmetic  0.92 us (1%)
    pallas_call x2, Pallas kernels, body(): pl.pallas_call(functools.partial(partial_kernel, (turn, group // CB, piec...  21.9 us
    ppermute x11, waiting for transfers between devices, swap(): return lax.ppermute(value, 'lm', [(i, i ^ 1 << bit) for i in range(n_lm)])  19.3 us
    ppermute x6, waiting for transfers between devices, body(): lax.ppermute(value, 'cam', [(i, i ^ pos + 1) for i in range(n_cam)])  13.8 us
    ppermute x6, starting transfers between devices, body(): lax.ppermute(value, 'cam', [(i, i ^ pos + 1) for i in range(n_cam)])  12.2 us
    ppermute x11, starting transfers between devices, swap(): return lax.ppermute(value, 'lm', [(i, i ^ 1 << bit) for i in range(n_lm)])  11.3 us
    pallas_call x2, Pallas kernels, body(): pl.pallas_call(functools.partial(finish_kernel, (turn, row_blocks, col_bl...  2.91 us
    unnamed x6, local copies, waits for them, and re-layouts  2.12 us
  transfers between devices with their start and end apart: 17, of which 7 were waited for; matrix products, arithmetic and copies ran while one was open for 1% of the time, Pallas kernels for 18%

profile of v2, /device:TPU:0, one launch (start us, length us, event | category | flops | bytes accessed | tf_op | source)
XLA Modules:
  0.0 86.7 jit_solution(4756802115951463475)
XLA Ops:
  0.0 0.5 collective-permute-start.1
  0.5 0.8 compare_select_fusion.ids_a
  1.2 0.1 collective-permute-start
  1.3 0.5 collective-permute-start.2
  1.7 0.1 pad_add_fusion.me_ref
  1.8 1.7 %collective-permute-done.ids_b = s32[2,16]{1,0:T(2,128)S(1)} collective-permute-done((s32[2,16]{1,0:T(2,128)S(1)}, s32[2,16]{1,0:T(2,128)S(1)}, u32[]{:S(2)}, u32[]{:S(2)}) %collective-permute-start) | collective-permute-done | bytes 160 | tf_op jit(solution)/shard_map/ppermute | solution.py:261
  3.5 0.2 collective-permute-done.2.cur_b
  3.7 0.0 collective-permute-done.1.pan_b
  3.7 0.0 copy-start
  3.7 1.4 %copy-done = bf16[2,16,64,384]{3,2,1,0:T(8,128)(2,1)S(1)} copy-done((bf16[2,16,64,384]{3,2,1,0:T(8,128)(2,1)S(1)}, bf16[2,16,64,384]{3,2,1,0:T(8,128)(2,1)}, u32[]{:S(2)}) %copy-start) | copy-done | bytes 1572888
  5.1 0.0 copy-start.1
  5.1 0.7 copy-done.1
  5.8 10.3 %partial.3 = (s16[2,272,512]{2,1,0:T(8,128)(2,1)S(1)}, s16[2,272,512]{2,1,0:T(8,128)(2,1)S(1)}, f32[2,256,512]{2,1,0:T(8,128)S(1)}, f32[2,256,512]{2,1,0:T(8,128)S(1)}) custom-call(s32[3]{0:T(128)S(1)} %pad_add_fusion.me_ref, s32[2,16]{1,0:T(2,128)S(1)} %compare_select_fusion.ids_a, s32[2,16]{1,0:T(2,128)S(1)} %collective-permute-done.ids_b, ...), custom_call_target="tpu_custom_call" | custom-call | tf_op jit(solution)/shard_map/partial/pallas_call | solution.py:271
  16.2 3.1 %collective-permute-start.10 = (s16[2,272,512]{2,1,0:T(8,128)(2,1)S(1)}, s16[2,272,512]{2,1,0:T(8,128)(2,1)S(1)}, u32[]{:S(2)}, u32[]{:S(2)}) collective-permute-start(s16[2,272,512]{2,1,0:T(8,128)(2,1)S(1)} %get-tuple-element.27), channel_id=1, source_target_pairs={{0,8},{4,12},{8,0},{12,4},{16,24},{20,28},{24,16},{28,20},{1,9},{5... | collective-permute-start | bytes 1671176 | tf_op jit(solution)/shard_map/ppermute | solution.py:261
  19.2 2.3 %collective-permute-start.12 = (s16[2,272,512]{2,1,0:T(8,128)(2,1)S(1)}, s16[2,272,512]{2,1,0:T(8,128)(2,1)S(1)}, u32[]{:S(2)}, u32[]{:S(2)}) collective-permute-start(s16[2,272,512]{2,1,0:T(8,128)(2,1)S(1)} %get-tuple-element.29), channel_id=1, source_target_pairs={{0,16},{4,20},{8,24},{12,28},{16,0},{20,4},{24,8},{28,12},{1,17},{... | collective-permute-start | bytes 1671176 | tf_op jit(solution)/shard_map/ppermute | solution.py:261
  21.5 11.6 %partial.2 = (s16[2,272,512]{2,1,0:T(8,128)(2,1)S(1)}, s16[2,272,512]{2,1,0:T(8,128)(2,1)S(1)}, f32[2,256,512]{2,1,0:T(8,128)S(1)}, f32[2,256,512]{2,1,0:T(8,128)S(1)}) custom-call(s32[3]{0:T(128)S(1)} %pad_add_fusion.me_ref, s32[2,16]{1,0:T(2,128)S(1)} %compare_select_fusion.ids_a, s32[2,16]{1,0:T(2,128)S(1)} %collective-permute-done.ids_b, ...), custom_call_target="tpu_custom_call" | custom-call | tf_op jit(solution)/shard_map/partial/pallas_call | solution.py:271
  33.1 2.2 %collective-permute-start.3 = (s16[2,272,512]{2,1,0:T(8,128)(2,1)S(1)}, s16[2,272,512]{2,1,0:T(8,128)(2,1)S(1)}, u32[]{:S(2)}, u32[]{:S(2)}) collective-permute-start(s16[2,272,512]{2,1,0:T(8,128)(2,1)S(1)} %get-tuple-element.20), channel_id=1, source_target_pairs={{0,8},{4,12},{8,0},{12,4},{16,24},{20,28},{24,16},{28,20},{1,9},{5... | collective-permute-start | bytes 1671176 | tf_op jit(solution)/shard_map/ppermute | solution.py:261
  35.3 0.0 collective-permute-start.5
  35.3 0.0 collective-permute-done.10.rest_0_.rest_1_
  35.3 0.3 relay.6
  35.6 2.1 %collective-permute-start.11 = (s16[1,272,512]{2,1,0:T(8,128)(2,1)S(1)}, s16[1,272,512]{2,1,0:T(8,128)(2,1)S(1)}, u32[]{:S(2)}, u32[]{:S(2)}) collective-permute-start(s16[1,272,512]{2,1,0:T(8,128)(2,1)S(1)} %relay.6), channel_id=1, source_target_pairs={{0,16},{4,20},{8,24},{12,28},{16,0},{20,4},{24,8},{28,12},{1,17},{... | collective-permute-start | bytes 835592 | tf_op jit(solution)/shard_map/ppermute | solution.py:261
  37.7 0.0 collective-permute-done.12.rest_0_.rest_4_
  37.7 0.3 relay.7
  38.1 0.1 collective-permute-start.13
  38.2 10.6 %collective-permute-done.3.rest_0_.rest_1_ = s16[2,272,512]{2,1,0:T(8,128)(2,1)S(1)} collective-permute-done((s16[2,272,512]{2,1,0:T(8,128)(2,1)S(1)}, s16[2,272,512]{2,1,0:T(8,128)(2,1)S(1)}, u32[]{:S(2)}, u32[]{:S(2)}) %collective-permute-start.3) | collective-permute-done | bytes 557088 | tf_op jit(solution)/shard_map/ppermute | solution.py:261
  48.8 0.3 relay.4
  49.2 0.1 collective-permute-start.4
  49.2 1.6 %collective-permute-done.5.rest_0_.rest_4_ = s16[2,272,512]{2,1,0:T(8,128)(2,1)S(1)} collective-permute-done((s16[2,272,512]{2,1,0:T(8,128)(2,1)S(1)}, s16[2,272,512]{2,1,0:T(8,128)(2,1)S(1)}, u32[]{:S(2)}, u32[]{:S(2)}) %collective-permute-start.5) | collective-permute-done | bytes 557088 | tf_op jit(solution)/shard_map/ppermute | solution.py:261
  50.8 0.3 relay.5
  51.2 0.5 collective-permute-start.6
  51.7 5.1 %collective-permute-done.11.rest_2_ = s16[1,272,512]{2,1,0:T(8,128)(2,1)S(1)} collective-permute-done((s16[1,272,512]{2,1,0:T(8,128)(2,1)S(1)}, s16[1,272,512]{2,1,0:T(8,128)(2,1)S(1)}, u32[]{:S(2)}, u32[]{:S(2)}) %collective-permute-start.11) | collective-permute-done | bytes 278560 | tf_op jit(solution)/shard_map/ppermute | solution.py:261
  56.8 0.0 collective-permute-done.13.rest_5_
  56.8 0.4 cross.3
  57.2 1.9 %collective-permute-start.14 = (s16[2,272,128]{2,1,0:T(8,128)(2,1)S(1)}, s16[2,272,128]{2,1,0:T(8,128)(2,1)S(1)}, u32[]{:S(2)}, u32[]{:S(2)}) collective-permute-start(s16[2,272,128]{2,1,0:T(8,128)(2,1)S(1)} %get-tuple-element.30), channel_id=1, source_target_pairs={{0,1},{1,0},{2,3},{3,2},{4,5},{5,4},{6,7},{7,6},{8,9},{9,8},{10,11... | collective-permute-start | bytes 417800 | tf_op jit(solution)/shard_map/ppermute | solution.py:352
  59.1 4.4 %collective-permute-start.15 = (s16[2,272,128]{2,1,0:T(8,128)(2,1)S(1)}, s16[2,272,128]{2,1,0:T(8,128)(2,1)S(1)}, u32[]{:S(2)}, u32[]{:S(2)}) collective-permute-start(s16[2,272,128]{2,1,0:T(8,128)(2,1)S(1)} %get-tuple-element.31), channel_id=1, source_target_pairs={{0,2},{1,3},{2,0},{3,1},{4,6},{5,7},{6,4},{7,5},{8,10},{9,11},{10,... | collective-permute-start | bytes 417800 | tf_op jit(solution)/shard_map/ppermute | solution.py:352
  63.5 0.0 copy-start.2
  63.5 0.0 collective-permute-start.16
  63.5 0.0 collective-permute-done.4.rest_2_
  63.5 0.0 collective-permute-done.6.rest_5_
  63.5 0.4 cross.2
  63.9 1.1 %collective-permute-start.7 = (s16[2,272,128]{2,1,0:T(8,128)(2,1)S(1)}, s16[2,272,128]{2,1,0:T(8,128)(2,1)S(1)}, u32[]{:S(2)}, u32[]{:S(2)}) collective-permute-start(s16[2,272,128]{2,1,0:T(8,128)(2,1)S(1)} %get-tuple-element.23), channel_id=1, source_target_pairs={{0,1},{1,0},{2,3},{3,2},{4,5},{5,4},{6,7},{7,6},{8,9},{9,8},{10,11... | collective-permute-start | bytes 417800 | tf_op jit(solution)/shard_map/ppermute | solution.py:352
  65.0 3.8 %collective-permute-start.8 = (s16[2,272,128]{2,1,0:T(8,128)(2,1)S(1)}, s16[2,272,128]{2,1,0:T(8,128)(2,1)S(1)}, u32[]{:S(2)}, u32[]{:S(2)}) collective-permute-start(s16[2,272,128]{2,1,0:T(8,128)(2,1)S(1)} %get-tuple-element.24), channel_id=1, source_target_pairs={{0,2},{1,3},{2,0},{3,1},{4,6},{5,7},{6,4},{7,5},{8,10},{9,11},{10,... | collective-permute-start | bytes 417800 | tf_op jit(solution)/shard_map/ppermute | solution.py:352
  68.8 0.0 collective-permute-done.14.rest_6_
  68.8 1.1 %collective-permute-start.9 = (s16[2,272,128]{2,1,0:T(8,128)(2,1)S(1)}, s16[2,272,128]{2,1,0:T(8,128)(2,1)S(1)}, u32[]{:S(2)}, u32[]{:S(2)}) collective-permute-start(s16[2,272,128]{2,1,0:T(8,128)(2,1)S(1)} %get-tuple-element.25), channel_id=1, source_target_pairs={{0,3},{1,2},{2,1},{3,0},{4,7},{5,6},{6,5},{7,4},{8,11},{9,10},{10,... | collective-permute-start | bytes 417800 | tf_op jit(solution)/shard_map/ppermute | solution.py:352
  69.9 0.0 copy-done.2
  69.9 0.1 pad_maximum_fusion.wide_ref
  70.0 4.1 %collective-permute-done.15.rest_7_ = s16[2,272,128]{2,1,0:T(8,128)(2,1)S(1)} collective-permute-done((s16[2,272,128]{2,1,0:T(8,128)(2,1)S(1)}, s16[2,272,128]{2,1,0:T(8,128)(2,1)S(1)}, u32[]{:S(2)}, u32[]{:S(2)}) %collective-permute-start.15) | collective-permute-done | bytes 139296 | tf_op jit(solution)/shard_map/ppermute | solution.py:352
  74.1 0.0 collective-permute-done.16.rest_8_
  74.1 1.5 %finish.2.rest_9_ = f32[256,512]{1,0:T(8,128)} custom-call(s32[3]{0:T(128)S(1)} %pad_add_fusion.me_ref, f32[4,64,128]{2,1,0:T(8,128)S(1)} %pad_maximum_fusion.wide_ref, f32[2,256,512]{2,1,0:T(8,128)S(1)} %get-tuple-element.26.keep_ref.rest_0_, s16[2,272,512]{2,1,0:T(8,128)(2,1)S(1)} %collective-permute-done.10.rest_0_.rest_1_, ...), custom_call_target="tpu_custom_call" | custom-call | tf_op jit(solution)/shard_map/finish/pallas_call | solution.py:356
  75.5 0.0 collective-permute-done.7.rest_6_
  75.5 9.8 %collective-permute-done.8.rest_7_ = s16[2,272,128]{2,1,0:T(8,128)(2,1)S(1)} collective-permute-done((s16[2,272,128]{2,1,0:T(8,128)(2,1)S(1)}, s16[2,272,128]{2,1,0:T(8,128)(2,1)S(1)}, u32[]{:S(2)}, u32[]{:S(2)}) %collective-permute-start.8) | collective-permute-done | bytes 139296 | tf_op jit(solution)/shard_map/ppermute | solution.py:352
  85.3 0.0 collective-permute-done.9.rest_8_
  85.3 1.5 %finish.3 = f32[256,512]{1,0:T(8,128)} custom-call(s32[3]{0:T(128)S(1)} %pad_add_fusion.me_ref, f32[4,64,128]{2,1,0:T(8,128)S(1)} %pad_maximum_fusion.wide_ref, f32[2,256,512]{2,1,0:T(8,128)S(1)} %get-tuple-element.19.keep_ref.rest_0_, s16[2,272,512]{2,1,0:T(8,128)(2,1)S(1)} %collective-permute-done.3.rest_0_.rest_1_, ...), custom_call_target="tpu_custom_call", output_to_operand_aliasing={{}: (11, {})} | custom-call | tf_op jit(solution)/shard_map/finish/pallas_call | solution.py:356
Async XLA Ops:
  0.0 3.7 %collective-permute-start.1 = (bf16[2,16,64,384]{3,2,1,0:T(8,128)(2,1)}, bf16[2,16,64,384]{3,2,1,0:T(8,128)(2,1)S(1)}, u32[]{:S(2)}, u32[]{:S(2)}) collective-permute-start(bf16[2,16,64,384]{3,2,1,0:T(8,128)(2,1)} %pan_a.3), channel_id=1, source_target_pairs={{0,4},{4,0},{8,12},{12,8},{16,20},{20,16},{24,28},{28,24},{1,5},{5... | collective-permute-start | bytes 4718600 | tf_op jit(solution)/shard_map/ppermute | solution.py:261
  1.2 2.3 %collective-permute-start = (s32[2,16]{1,0:T(2,128)S(1)}, s32[2,16]{1,0:T(2,128)S(1)}, u32[]{:S(2)}, u32[]{:S(2)}) collective-permute-start(s32[2,16]{1,0:T(2,128)S(1)} %compare_select_fusion.ids_a), channel_id=1, source_target_pairs={{0,4},{4,0},{8,12},{12,8},{16,20},{20,16},{24,28},{28,24},{1,5},{5... | collective-permute-start | bytes 392 | tf_op jit(solution)/shard_map/ppermute | solution.py:261
  1.3 2.5 %collective-permute-start.2 = (f32[3,3,256]{2,1,0:T(4,128)}, f32[3,3,256]{2,1,0:T(4,128)S(1)}, u32[]{:S(2)}, u32[]{:S(2)}) collective-permute-start(f32[3,3,256]{2,1,0:T(4,128)} %cur_a.3), channel_id=1, source_target_pairs={{0,4},{4,0},{8,12},{12,8},{16,20},{20,16},{24,28},{28,24},{1,5},{5... | collective-permute-start | bytes 27656 | tf_op jit(solution)/shard_map/ppermute | solution.py:261
  3.7 1.4 %copy-start = (bf16[2,16,64,384]{3,2,1,0:T(8,128)(2,1)S(1)}, bf16[2,16,64,384]{3,2,1,0:T(8,128)(2,1)}, u32[]{:S(2)}) copy-start(bf16[2,16,64,384]{3,2,1,0:T(8,128)(2,1)} %pan_a.3) | copy-start | bytes 4718596
  5.1 0.7 copy-start.1
  16.2 19.1 %collective-permute-start.10 = (s16[2,272,512]{2,1,0:T(8,128)(2,1)S(1)}, s16[2,272,512]{2,1,0:T(8,128)(2,1)S(1)}, u32[]{:S(2)}, u32[]{:S(2)}) collective-permute-start(s16[2,272,512]{2,1,0:T(8,128)(2,1)S(1)} %get-tuple-element.27), channel_id=1, source_target_pairs={{0,8},{4,12},{8,0},{12,4},{16,24},{20,28},{24,16},{28,20},{1,9},{5... | collective-permute-start | bytes 1671176 | tf_op jit(solution)/shard_map/ppermute | solution.py:261
  19.2 18.5 %collective-permute-start.12 = (s16[2,272,512]{2,1,0:T(8,128)(2,1)S(1)}, s16[2,272,512]{2,1,0:T(8,128)(2,1)S(1)}, u32[]{:S(2)}, u32[]{:S(2)}) collective-permute-start(s16[2,272,512]{2,1,0:T(8,128)(2,1)S(1)} %get-tuple-element.29), channel_id=1, source_target_pairs={{0,16},{4,20},{8,24},{12,28},{16,0},{20,4},{24,8},{28,12},{1,17},{... | collective-permute-start | bytes 1671176 | tf_op jit(solution)/shard_map/ppermute | solution.py:261
  33.1 15.7 %collective-permute-start.3 = (s16[2,272,512]{2,1,0:T(8,128)(2,1)S(1)}, s16[2,272,512]{2,1,0:T(8,128)(2,1)S(1)}, u32[]{:S(2)}, u32[]{:S(2)}) collective-permute-start(s16[2,272,512]{2,1,0:T(8,128)(2,1)S(1)} %get-tuple-element.20), channel_id=1, source_target_pairs={{0,8},{4,12},{8,0},{12,4},{16,24},{20,28},{24,16},{28,20},{1,9},{5... | collective-permute-start | bytes 1671176 | tf_op jit(solution)/shard_map/ppermute | solution.py:261
  35.3 15.6 %collective-permute-start.5 = (s16[2,272,512]{2,1,0:T(8,128)(2,1)S(1)}, s16[2,272,512]{2,1,0:T(8,128)(2,1)S(1)}, u32[]{:S(2)}, u32[]{:S(2)}) collective-permute-start(s16[2,272,512]{2,1,0:T(8,128)(2,1)S(1)} %get-tuple-element.22), channel_id=1, source_target_pairs={{0,16},{4,20},{8,24},{12,28},{16,0},{20,4},{24,8},{28,12},{1,17},{... | collective-permute-start | bytes 1671176 | tf_op jit(solution)/shard_map/ppermute | solution.py:261
  35.6 21.2 %collective-permute-start.11 = (s16[1,272,512]{2,1,0:T(8,128)(2,1)S(1)}, s16[1,272,512]{2,1,0:T(8,128)(2,1)S(1)}, u32[]{:S(2)}, u32[]{:S(2)}) collective-permute-start(s16[1,272,512]{2,1,0:T(8,128)(2,1)S(1)} %relay.6), channel_id=1, source_target_pairs={{0,16},{4,20},{8,24},{12,28},{16,0},{20,4},{24,8},{28,12},{1,17},{... | collective-permute-start | bytes 835592 | tf_op jit(solution)/shard_map/ppermute | solution.py:261
  38.1 18.8 %collective-permute-start.13 = (s16[1,272,512]{2,1,0:T(8,128)(2,1)S(1)}, s16[1,272,512]{2,1,0:T(8,128)(2,1)S(1)}, u32[]{:S(2)}, u32[]{:S(2)}) collective-permute-start(s16[1,272,512]{2,1,0:T(8,128)(2,1)S(1)} %relay.7), channel_id=1, source_target_pairs={{0,8},{4,12},{8,0},{12,4},{16,24},{20,28},{24,16},{28,20},{1,9},{5... | collective-permute-start | bytes 835592 | tf_op jit(solution)/shard_map/ppermute | solution.py:261
  49.2 14.3 %collective-permute-start.4 = (s16[1,272,512]{2,1,0:T(8,128)(2,1)S(1)}, s16[1,272,512]{2,1,0:T(8,128)(2,1)S(1)}, u32[]{:S(2)}, u32[]{:S(2)}) collective-permute-start(s16[1,272,512]{2,1,0:T(8,128)(2,1)S(1)} %relay.4), channel_id=1, source_target_pairs={{0,16},{4,20},{8,24},{12,28},{16,0},{20,4},{24,8},{28,12},{1,17},{... | collective-permute-start | bytes 835592 | tf_op jit(solution)/shard_map/ppermute | solution.py:261
  51.2 12.3 %collective-permute-start.6 = (s16[1,272,512]{2,1,0:T(8,128)(2,1)S(1)}, s16[1,272,512]{2,1,0:T(8,128)(2,1)S(1)}, u32[]{:S(2)}, u32[]{:S(2)}) collective-permute-start(s16[1,272,512]{2,1,0:T(8,128)(2,1)S(1)} %relay.5), channel_id=1, source_target_pairs={{0,8},{4,12},{8,0},{12,4},{16,24},{20,28},{24,16},{28,20},{1,9},{5... | collective-permute-start | bytes 835592 | tf_op jit(solution)/shard_map/ppermute | solution.py:261
  57.2 11.6 %collective-permute-start.14 = (s16[2,272,128]{2,1,0:T(8,128)(2,1)S(1)}, s16[2,272,128]{2,1,0:T(8,128)(2,1)S(1)}, u32[]{:S(2)}, u32[]{:S(2)}) collective-permute-start(s16[2,272,128]{2,1,0:T(8,128)(2,1)S(1)} %get-tuple-element.30), channel_id=1, source_target_pairs={{0,1},{1,0},{2,3},{3,2},{4,5},{5,4},{6,7},{7,6},{8,9},{9,8},{10,11... | collective-permute-start | bytes 417800 | tf_op jit(solution)/shard_map/ppermute | solution.py:352
  59.1 15.0 %collective-permute-start.15 = (s16[2,272,128]{2,1,0:T(8,128)(2,1)S(1)}, s16[2,272,128]{2,1,0:T(8,128)(2,1)S(1)}, u32[]{:S(2)}, u32[]{:S(2)}) collective-permute-start(s16[2,272,128]{2,1,0:T(8,128)(2,1)S(1)} %get-tuple-element.31), channel_id=1, source_target_pairs={{0,2},{1,3},{2,0},{3,1},{4,6},{5,7},{6,4},{7,5},{8,10},{9,11},{10,... | collective-permute-start | bytes 417800 | tf_op jit(solution)/shard_map/ppermute | solution.py:352
  63.5 6.4 %copy-start.2 = (f32[4,64,64]{2,1,0:T(8,128)S(1)}, f32[4,64,64]{2,1,0:T(8,128)}, u32[]{:S(2)}) copy-start(f32[4,64,64]{2,1,0:T(8,128)} %param.9) | copy-start | bytes 196612
  63.5 10.6 %collective-permute-start.16 = (s16[2,272,128]{2,1,0:T(8,128)(2,1)S(1)}, s16[2,272,128]{2,1,0:T(8,128)(2,1)S(1)}, u32[]{:S(2)}, u32[]{:S(2)}) collective-permute-start(s16[2,272,128]{2,1,0:T(8,128)(2,1)S(1)} %get-tuple-element.32), channel_id=1, source_target_pairs={{0,3},{1,2},{2,1},{3,0},{4,7},{5,6},{6,5},{7,4},{8,11},{9,10},{10,... | collective-permute-start | bytes 417800 | tf_op jit(solution)/shard_map/ppermute | solution.py:352
  63.9 11.7 %collective-permute-start.7 = (s16[2,272,128]{2,1,0:T(8,128)(2,1)S(1)}, s16[2,272,128]{2,1,0:T(8,128)(2,1)S(1)}, u32[]{:S(2)}, u32[]{:S(2)}) collective-permute-start(s16[2,272,128]{2,1,0:T(8,128)(2,1)S(1)} %get-tuple-element.23), channel_id=1, source_target_pairs={{0,1},{1,0},{2,3},{3,2},{4,5},{5,4},{6,7},{7,6},{8,9},{9,8},{10,11... | collective-permute-start | bytes 417800 | tf_op jit(solution)/shard_map/ppermute | solution.py:352
  65.0 20.3 %collective-permute-start.8 = (s16[2,272,128]{2,1,0:T(8,128)(2,1)S(1)}, s16[2,272,128]{2,1,0:T(8,128)(2,1)S(1)}, u32[]{:S(2)}, u32[]{:S(2)}) collective-permute-start(s16[2,272,128]{2,1,0:T(8,128)(2,1)S(1)} %get-tuple-element.24), channel_id=1, source_target_pairs={{0,2},{1,3},{2,0},{3,1},{4,6},{5,7},{6,4},{7,5},{8,10},{9,11},{10,... | collective-permute-start | bytes 417800 | tf_op jit(solution)/shard_map/ppermute | solution.py:352
  68.8 16.5 %collective-permute-start.9 = (s16[2,272,128]{2,1,0:T(8,128)(2,1)S(1)}, s16[2,272,128]{2,1,0:T(8,128)(2,1)S(1)}, u32[]{:S(2)}, u32[]{:S(2)}) collective-permute-start(s16[2,272,128]{2,1,0:T(8,128)(2,1)S(1)} %get-tuple-element.25), channel_id=1, source_target_pairs={{0,3},{1,2},{2,1},{3,0},{4,7},{5,6},{6,5},{7,4},{8,11},{9,10},{10,... | collective-permute-start | bytes 417800 | tf_op jit(solution)/shard_map/ppermute | solution.py:352

commit v3 on v0

v3 whole, which is shorter than its diff:
```python
import functools
import math

import jax
import jax.numpy as jnp
from jax import lax
from jax.experimental import pallas as pl
from jax.experimental.pallas import tpu as pltpu
from jax.sharding import PartitionSpec as P

CB = 64
LMB = 128
K = 16
WIDTH = 3 * LMB
LANES = 128
QUAD = 4
VMEM = pl.BlockSpec(memory_space=pltpu.VMEM)
SMEM = pl.BlockSpec(memory_space=pltpu.SMEM)
PARAMS = pltpu.CompilerParams(vmem_limit_bytes=32 * 1024 * 1024)


def invert_rows(cur_ref, start):
    lanes = pl.ds(start, LMB)
    entry = [[cur_ref[row, col : col + 1, lanes] for col in range(3)] for row in range(3)]
    cofactor = [
        [
            entry[(row + 1) % 3][(col + 1) % 3] * entry[(row + 2) % 3][(col + 2) % 3]
            - entry[(row + 1) % 3][(col + 2) % 3] * entry[(row + 2) % 3][(col + 1) % 3]
            for col in range(3)
        ]
        for row in range(3)
    ]
    determ = (
        entry[0][0] * cofactor[0][0] + entry[0][1] * cofactor[0][1] + entry[0][2] * cofactor[0][2]
    )
    return [[cofactor[col][row] / determ for col in range(3)] for row in range(3)]


def strip_of(blocks):
    return -(-blocks // 16) * 16


def encode(dst, lanes, parts):
    blocks = len(parts)
    strip = strip_of(blocks)
    row = lax.broadcasted_iota(jnp.int32, (strip, LANES), 0)
    tops = jnp.full((strip, LANES), 2.0**-100, jnp.float32)
    for block, part in enumerate(parts):
        top = jnp.max(jnp.abs(part()), axis=0, keepdims=True)
        tops = jnp.where(row == block, jnp.maximum(top, tops), tops)
    power = jnp.ceil(jnp.log2(tops) - 14.99)
    inverse = jnp.exp2(-power)
    for block, part in enumerate(parts):
        coded = jnp.floor(part() * inverse[block : block + 1] + 0.5)
        dst[pl.ds(block * CB, CB), lanes] = coded.astype(jnp.int32).astype(jnp.int16)
    dst[pl.ds(blocks * CB, strip), lanes] = power.astype(jnp.int32).astype(jnp.int16)


def scales(src, lanes):
    blocks = src.shape[0] // CB
    strip = src[pl.ds(blocks * CB, strip_of(blocks)), lanes]
    return jnp.exp2(strip.astype(jnp.int32).astype(jnp.float32))


def decode(src, lanes, scale, block):
    coded = src[pl.ds(block * CB, CB), lanes].astype(jnp.int32).astype(jnp.float32)
    return coded * scale[block : block + 1]


def gathered(keep, came, lanes, first, place, blocks):
    parts = [keep[pl.ds(first + block * CB, CB), lanes] for block in range(blocks)]
    for src in came:
        scale = scales(src, lanes)
        parts = [
            part + decode(src, lanes, scale, place * blocks + block)
            for block, part in enumerate(parts)
        ]
    return parts


def given(values):
    return [functools.partial(lambda value: value, value) for value in values]


def index_of(spot, order):
    bits = len(order)
    return sum(((spot >> bit) & 1) << (bits - 1 - pos) for pos, bit in enumerate(order))


def place_of(spot, block, orders, half_blocks, halves):
    half = block // half_blocks
    index = index_of(spot, orders[half])
    region = 0 if index >= halves else 1
    row = (half * halves + index % halves) * half_blocks + block % half_blocks
    return region * 2 * halves * half_blocks + row


def form_tile(plan, table, tile, pan, cur, rows, line_at, many):
    total, region_size = plan
    inverse = invert_rows(cur, tile * LMB)
    for region in range(2):
        list_at = region * (region_size + QUAD)

        def one_place(place, count):
            slot = table[tile, total + region * region_size + place]

            @pl.when(slot >= 0)
            def form():
                line_at[tile, list_at + count] = (region * region_size + place) * CB
                lines = pl.ds(pl.multiple_of((region * region_size + count) * CB, CB), CB)
                wide = pan[tile, slot].astype(jnp.float32)
                split = [wide[:, c * LMB : (c + 1) * LMB] for c in range(3)]
                for q in range(3):
                    formed = (
                        split[0] * inverse[0][q]
                        + split[1] * inverse[1][q]
                        + split[2] * inverse[2][q]
                    )
                    high = formed.astype(jnp.bfloat16)
                    low = (formed - high.astype(jnp.float32)).astype(jnp.bfloat16)
                    at = q * LMB
                    rows[tile, lines, at : at + LMB] = high
                    rows[tile, lines, WIDTH + at : WIDTH + at + LMB] = low

            return count + jnp.where(slot >= 0, 1, 0)

        count = lax.fori_loop(0, region_size, one_place, jnp.int32(0))
        many[tile, region] = (count + QUAD - 1) // QUAD
        for extra in range(QUAD):
            line_at[tile, list_at + count + extra] = 2 * region_size * CB


def form_own_kernel(plan, table, pan_ref, cur_ref, rows, line_at, many, pan, cur, sems):
    tiles = rows.shape[0]
    copies = [
        pltpu.make_async_copy(pan_ref.at[tile], pan.at[tile], sems.at[tile])
        for tile in range(tiles)
    ]
    small = pltpu.make_async_copy(cur_ref, cur, sems.at[tiles])
    small.start()
    for copy in copies:
        copy.start()
    small.wait()
    for tile, copy in enumerate(copies):
        copy.wait()
        form_tile(plan, table, tile, pan, cur, rows, line_at, many)


def form_kernel(plan, table, pan, cur, rows, line_at, many):
    for tile in range(rows.shape[0]):
        form_tile(plan, table, tile, pan, cur, rows, line_at, many)


def accumulate(plan, sides, right, pair_at, acc):
    base, pairs, regions, region_size = plan
    acc[...] = jnp.zeros_like(acc)
    dump = acc.shape[0] - CB
    for table, line_at, many, pan, rows in sides:

        def one_tile(tile, carry):
            used = functools.reduce(jnp.maximum, [many[tile, region] for region in regions])

            @pl.when(used > 0)
            def some():
                def one_pair(pair, count):
                    slots = [table[tile, base + 2 * pair + side] for side in range(2)]
                    live = jnp.maximum(slots[0], slots[1]) >= 0

                    @pl.when(live)
                    def stage():
                        pair_at[count] = pair * LANES
                        for side, slot in enumerate(slots):
                            first = pl.multiple_of(count * LANES + side * CB, CB)
                            lines = pl.ds(first, CB)

                            @pl.when(slot >= 0)
                            def fill():
                                panel = pan[tile, slot]
                                right[lines, :WIDTH] = panel
                                right[lines, WIDTH:] = panel

                            @pl.when(slot < 0)
                            def blank():
                                right[lines, :] = jnp.zeros((CB, 2 * WIDTH), jnp.bfloat16)

                    return count + jnp.where(live, 1, 0)

                count = lax.fori_loop(0, pairs, one_pair, jnp.int32(0))
                pair_at[count] = pairs * LANES
                for region in regions:
                    shift = region * region_size * CB if len(regions) == 1 else 0

                    def one_group(group, carry):
                        start = (region * region_size + group * QUAD) * CB
                        lines = pl.ds(pl.multiple_of(start, QUAD * CB), QUAD * CB)
                        list_at = region * (region_size + QUAD) + group * QUAD

                        def one_dot(double, carry):
                            first = pl.multiple_of(double * 2 * LANES, 2 * LANES)
                            result = lax.dot_general(
                                rows[tile, lines, :],
                                right[pl.ds(first, 2 * LANES), :],
                                (((1,), (1,)), ((), ())),
                                preferred_element_type=jnp.float32,
                            )
                            for block in range(QUAD):
                                line = jnp.minimum(line_at[tile, list_at + block] - shift, dump)
                                line = pl.multiple_of(line, CB)
                                for side in range(2):
                                    lane = pl.multiple_of(pair_at[2 * double + side], LANES)
                                    acc[pl.ds(line, CB), pl.ds(lane, LANES)] += result[
                                        block * CB : (block + 1) * CB,
                                        side * LANES : (side + 1) * LANES,
                                    ]
                            return carry

                        return lax.fori_loop(0, (count + 1) // 2, one_dot, carry)

                    lax.fori_loop(0, many[tile, region], one_group, 0)

            return carry

        lax.fori_loop(0, rows.shape[0], one_tile, 0)


def each_tile(columns, work):
    def one(start, carry):
        work(pl.ds(pl.multiple_of(start * LANES, LANES), LANES))
        return carry

    lax.fori_loop(0, columns // LANES, one, 0)


def blocks_at(acc, first, blocks, lanes):
    return [
        functools.partial(lambda block: acc[pl.ds(first + block * CB, CB), lanes], block)
        for block in range(blocks)
    ]


def sides_of(refs):
    return [refs[:5], refs[5:10]]


def send_kernel(plan, *refs):
    outs, (right, pair_at, acc) = refs[10:12], refs[12:]
    accumulate(plan, sides_of(refs), right, pair_at, acc)
    blocks = plan[3] // 2

    def code(lanes):
        for half, out in enumerate(outs):
            encode(out, lanes, blocks_at(acc, half * blocks * CB, blocks, lanes))

    each_tile(outs[0].shape[1], code)


def keep_kernel(plan, *refs):
    acc, right, pair_at = refs[10:]
    accumulate(plan, sides_of(refs), right, pair_at, acc)


def chain_kernel(plan, *refs):
    acc, to_right, to_left, right, pair_at = refs[10:]
    accumulate(plan, sides_of(refs), right, pair_at, acc)
    _, n_cam, _, region_size = plan
    for group, out in ((n_cam - 1, to_right), (1, to_left)):
        lanes = pl.ds(group * LANES, LANES)
        encode(out, pl.ds(0, LANES), blocks_at(acc, 0, 2 * region_size, lanes))


def link_kernel(groups, acc, from_left, from_right, to_right, to_left):
    for group, src, out in zip(groups, (from_left, from_right), (to_right, to_left)):
        blocks = src.shape[0] // CB
        here = pl.ds(0, LANES)
        lanes = pl.ds(group * LANES, LANES)
        scale = scales(src, here)
        parts = [
            functools.partial(
                lambda block, src, lanes, scale: acc[pl.ds(block * CB, CB), lanes]
                + decode(src, here, scale, block),
                block,
                src,
                lanes,
                scale,
            )
            for block in range(blocks)
        ]
        encode(out, here, parts)


def spread_kernel(places, acc, from_left, from_right, *outs):
    here = pl.ds(0, LANES)
    left, right = scales(from_left, here), scales(from_right, here)
    for spot, out in enumerate(outs):
        parts = [
            acc[pl.ds(place * CB, CB), here]
            + decode(from_left, here, left, place)
            + decode(from_right, here, right, place)
            for place in places[spot]
        ]
        if spot:
            encode(out, here, given(parts))
        else:
            for block, part in enumerate(parts):
                out[pl.ds(block * CB, CB), :] = part


def relay_kernel(plan, keep, *rest):
    first, blocks, size = plan
    dst = rest[-1]

    def code(lanes):
        parts = []
        for place in range(size // 2, size):
            line = first + place * blocks * CB
            parts += given(gathered(keep, rest[:-1], lanes, line, place, blocks))
        encode(dst, lanes, parts)

    each_tile(dst.shape[1], code)


def own_rows(firsts, blocks, keep, came, lanes):
    parts = []
    for first, arrays in zip(firsts, came):
        parts += gathered(keep, arrays, lanes, first, 0, blocks)
    return parts


def cross_kernel(plan, keep, *rest):
    firsts, blocks, arrays = plan
    came = [rest[half * arrays : (half + 1) * arrays] for half in range(2)]
    dsts = rest[2 * arrays :]
    group = dsts[0].shape[1]
    for other, dst in enumerate(dsts):

        def code(start, carry, other=other, dst=dst):
            at = pl.multiple_of(start * LANES, LANES)
            lanes = pl.ds(pl.multiple_of((other + 1) * group + at, LANES), LANES)
            encode(dst, pl.ds(at, LANES), given(own_rows(firsts, blocks, keep, came, lanes)))
            return carry

        lax.fori_loop(0, group // LANES, code, 0)


def hessian_part(me_ref, wide_ref, plan, start, block):
    row_blocks, col_blocks = plan
    row = (me_ref[0] * 2 + me_ref[1]) * row_blocks + block
    lane = lax.broadcasted_iota(jnp.int32, (CB, LANES), 1) // CB
    return jnp.where(me_ref[2] * col_blocks + start // CB + lane == row, wide_ref[block], 0.0)


def base_kernel(plan, me_ref, wide_ref, keep, *rest):
    sizes, firsts, blocks, arrays = plan
    came = [rest[half * arrays : (half + 1) * arrays] for half in range(2)]
    out = rest[-1]
    for start in range(0, out.shape[1], LANES):
        lanes = pl.ds(start, LANES)
        for block, part in enumerate(own_rows(firsts, blocks, keep, came, lanes)):
            out[pl.ds(block * CB, CB), lanes] = (
                hessian_part(me_ref, wide_ref, sizes, start, block) - part
            )


def small_kernel(plan, me_ref, wide_ref, own, *rest):
    sizes, start = plan
    out = rest[-1]
    here = pl.ds(0, LANES)
    parts = gathered(own, rest[:-1], here, 0, 0, sizes[0])
    for block, part in enumerate(parts):
        out[pl.ds(block * CB, CB), :] = hessian_part(me_ref, wide_ref, sizes, start, block) - part


def finish_kernel(blocks, base, small, *rest):
    out = rest[-1]
    step = pl.program_id(0)
    last = base.shape[1] // LANES

    @pl.when(step < last)
    def large():
        lanes = pl.ds(pl.multiple_of(step * LANES, LANES), LANES)
        factors = [scales(src, lanes) for src in rest[:-1]]
        for block in range(blocks):
            total = base[pl.ds(block * CB, CB), lanes]
            for src, scale in zip(rest[:-1], factors):
                total = total - decode(src, lanes, scale, block)
            out[pl.ds(block * CB, CB), :] = total

    @pl.when(step == last)
    def rest_of_it():
        out[...] = small[...]


def body(panels, curvature, visible_blocks, counts, camera_hessian):
    tiles = panels.shape[0]
    n_lm, n_cam = lax.axis_size("lm"), lax.axis_size("cam")
    chips = n_lm // 2
    halves = chips // 2
    bits = int(math.log2(chips))
    row_blocks = camera_hessian.shape[0]
    half_blocks = row_blocks // 2
    extent = row_blocks * CB
    total = row_blocks * n_lm
    col_blocks = total // n_cam
    large = col_blocks * CB - LANES
    per = large // CB
    columns = large * n_cam
    region_size = chips * half_blocks
    orders = [list(range(bits)), list(reversed(range(bits)))]
    lm, cam = lax.axis_index("lm"), lax.axis_index("cam")
    me = jnp.stack([lm // 2, lm % 2, cam]).astype(jnp.int32)

    live = jnp.arange(K, dtype=jnp.int32)[None, :] < counts[:, None]
    ids = jnp.where(live, visible_blocks, -1)

    def swap(value, step):
        return lax.ppermute(value, "lm", [(i, i ^ step) for i in range(n_lm)])

    pan_other, cur_other, ids_other = swap(panels, 1), swap(curvature, 1), swap(ids, 1)
    wide = jnp.concatenate([camera_hessian, camera_hessian], axis=-1)
    slots = jnp.arange(K, dtype=jnp.int32)[None, :, None]
    places = jnp.arange(total + 2 * region_size, dtype=jnp.int32)

    def table_of(ids):
        inner, owner = ids % col_blocks, ids // col_blocks
        spot = jnp.where(
            inner < per,
            (owner ^ cam) * per + inner,
            n_cam * per + ((owner - cam) % n_cam) * (col_blocks - per) + inner - per,
        )
        owner = ids // row_blocks
        group, block = (owner // 2) ^ (lm // 2), ids % row_blocks
        half = block // half_blocks
        index = jnp.where(half == 0, index_of(group, orders[0]), index_of(group, orders[1]))
        line = (half * halves + index % halves) * half_blocks + block % half_blocks
        line = total + line + jnp.where(index >= halves, 0, region_size)
        spot = jnp.where(ids >= 0, spot, -1)
        line = jnp.where((ids >= 0) & (owner % 2 == lm % 2), line, -1)
        found = (spot[:, :, None] == places) | (line[:, :, None] == places)
        return jnp.max(jnp.where(found, slots, -1), axis=1)

    def call(kernel, name, outs, scratch=(), **options):
        return pl.pallas_call(
            kernel,
            out_shape=outs,
            scratch_shapes=list(scratch),
            compiler_params=PARAMS,
            name=name,
            **options,
        )

    def coded(blocks, columns):
        return jax.ShapeDtypeStruct((blocks * CB + strip_of(blocks), columns), jnp.int16)

    def exact(rows, columns):
        return jax.ShapeDtypeStruct((rows, columns), jnp.float32)

    table_a, table_b = table_of(ids), table_of(ids_other)
    formed = [
        jax.ShapeDtypeStruct((tiles, 2 * region_size * CB, 2 * WIDTH), jnp.bfloat16),
        jax.ShapeDtypeStruct((tiles, 2 * (region_size + QUAD)), jnp.int32),
        jax.ShapeDtypeStruct((tiles, 2), jnp.int32),
    ]
    in_hbm = pl.BlockSpec(memory_space=pltpu.HBM)
    rows_a, line_a, many_a, pan_here = call(
        functools.partial(form_own_kernel, (total, region_size)),
        "form_own",
        formed + [jax.ShapeDtypeStruct(panels.shape, panels.dtype)],
        [pltpu.VMEM(curvature.shape, jnp.float32), pltpu.SemaphoreType.DMA((tiles + 1,))],
        in_specs=[SMEM, in_hbm, in_hbm],
        out_specs=[VMEM, SMEM, SMEM, VMEM],
    )(table_a, panels, curvature)
    rows_b, line_b, many_b = call(
        functools.partial(form_kernel, (total, region_size)),
        "form_other",
        formed,
        in_specs=[SMEM, VMEM, VMEM],
        out_specs=[VMEM, SMEM, SMEM],
    )(table_b, pan_other, cur_other)

    def scratch(pairs):
        return [
            pltpu.VMEM(((pairs + 1) * LANES, 2 * WIDTH), jnp.bfloat16),
            pltpu.SMEM((pairs + 1,), jnp.int32),
        ]

    def sums(kernel, name, base, pairs, regions, outs, more, tables):
        plan = (base, pairs, regions, region_size)
        side = [SMEM] * 3 + [VMEM] * 2
        return call(
            functools.partial(kernel, plan),
            name,
            outs,
            scratch(pairs) + more,
            in_specs=side * 2,
            out_specs=[VMEM] * len(outs),
        )(tables[0], line_a, many_a, pan_here, rows_a, tables[1], line_b, many_b, pan_other, rows_b)

    tables = (table_a, table_b)
    pairs = columns // LANES
    sum_shape = ((region_size + 1) * CB, columns + LANES)
    sends = sums(
        send_kernel,
        "send",
        0,
        pairs,
        [0],
        [coded(halves * half_blocks, columns)] * 2,
        [pltpu.VMEM(sum_shape, jnp.float32)],
        tables,
    )
    tables = lax.optimization_barrier((tables, sends))[0]
    acc, to_right, to_left = sums(
        chain_kernel,
        "chain",
        n_cam * per,
        n_cam,
        [0, 1],
        [exact((2 * region_size + 1) * CB, (n_cam + 1) * LANES)]
        + [coded(2 * region_size, LANES)] * 2,
        [],
        tables,
    )
    tables = lax.optimization_barrier((tables, acc))[0]
    (keep,) = sums(keep_kernel, "keep", 0, pairs, [1], [exact(*sum_shape)], [], tables)

    links = []
    for step in range(n_cam - 1):
        from_left = lax.ppermute(to_right, "cam", [(i, i + 1) for i in range(step + 1)])
        from_right = lax.ppermute(
            to_left, "cam", [(i, i - 1) for i in range(n_cam - 1 - step, n_cam)]
        )
        links.append((from_left, from_right))
        if step < n_cam - 2:
            groups = (n_cam - 2 - step, step + 2)
            to_right, to_left = call(
                functools.partial(link_kernel, groups),
                "link",
                [coded(2 * region_size, LANES)] * 2,
                in_specs=[VMEM] * 3,
                out_specs=[VMEM] * 2,
            )(acc, from_left, from_right)

    came = [[], []]
    firsts = [half * halves * half_blocks * CB for half in range(2)]
    for stage in range(bits):
        for half in range(2):
            came[half].append(swap(sends[half], 2 << orders[half][stage]))
        size = chips >> (stage + 1)
        if size == 1:
            break
        keep_now = lax.optimization_barrier((keep, links[min(n_cam - 3, 1)]))[0]
        sends = [
            call(
                functools.partial(relay_kernel, (firsts[half], half_blocks, size)),
                "relay",
                coded(size // 2 * half_blocks, columns),
                in_specs=[VMEM] * (1 + len(came[half])),
                out_specs=VMEM,
            )(keep_now, *came[half])
            for half in range(2)
        ]

    near = came[0] + came[1]
    sizes = (row_blocks, col_blocks)
    crossed = call(
        functools.partial(cross_kernel, (firsts, half_blocks, bits)),
        "cross",
        [coded(row_blocks, large)] * (n_cam - 1),
        in_specs=[VMEM] * (1 + len(near)),
        out_specs=[VMEM] * (n_cam - 1),
    )(keep, *near)
    far = [
        lax.ppermute(value, "cam", [(i, i ^ (pos + 1)) for i in range(n_cam)])
        for pos, value in enumerate(crossed)
    ]
    base = call(
        functools.partial(base_kernel, (sizes, firsts, half_blocks, bits)),
        "base",
        exact(extent, large),
        in_specs=[SMEM] + [VMEM] * (2 + len(near)),
        out_specs=VMEM,
    )(me, wide, keep, *near)

    spots = [
        [place_of(spot, block, orders, half_blocks, halves) for block in range(row_blocks)]
        for spot in range(chips)
    ]
    ends = lax.optimization_barrier((links[-1], crossed))[0]
    own, *spread = call(
        functools.partial(spread_kernel, spots),
        "spread",
        [exact(extent, LANES)] + [coded(row_blocks, LANES)] * (chips - 1),
        in_specs=[VMEM] * 3,
        out_specs=[VMEM] * chips,
    )(acc, *ends)
    others = [swap(value, 2 * (pos + 1)) for pos, value in enumerate(spread)]
    small = call(
        functools.partial(small_kernel, (sizes, large)),
        "small",
        exact(extent, LANES),
        in_specs=[SMEM] + [VMEM] * (2 + len(others)),
        out_specs=VMEM,
    )(me, wide, own, *others)
    return call(
        functools.partial(finish_kernel, row_blocks),
        "finish",
        exact(extent, col_blocks * CB),
        grid=(col_blocks * CB // LANES,),
        in_specs=[VMEM] * (1 + n_cam),
        out_specs=pl.BlockSpec((extent, LANES), lambda step: (0, step)),
    )(base, small, *far)


def solution(mesh):
    return jax.shard_map(
        body,
        mesh=mesh,
        in_specs=(
            P(("lm", "cam"), None, None, None),
            P(None, None, ("lm", "cam")),
            P(("lm", "cam"), None),
            P(("lm", "cam")),
            P("lm", None, None),
        ),
        out_specs=P("lm", "cam"),
        check_vma=False,
    )
```

time: 453 us -> 84.6 us (0.19); the launches traced: 449 us -> 85.3 us
  local copies, waits for them, and re-layouts: 149 us -> 2.12 us
  other arithmetic: 135 us -> 1.21 us
  waiting for transfers between devices: 92.8 us -> 15.1 us
  starting transfers between devices: 0.04 us -> 38.7 us
  matrix products: 36.7 us -> 0 us
  Pallas kernels: 0 us -> 27.8 us
  blocking collectives: 20.6 us -> 0 us
  between operations: 13.6 us -> 0.25 us
    all_gather x1 -> x0, waiting for transfers between devices: 54.6 us -> none  [body(): piece_panels = lax.all_gather(masked, 'lm', axis=0, tiled=True)]
    add x16 -> x0, other arithmetic: 41.9 us -> none  [form_panel(): split[..., 0, :] * inverse[0, target]]
    convert_element_type x16 -> x0, local copies, waits for them, and re-layouts: 39.9 us -> none  [form_panel(): block_panel.astype(jnp.float32).reshape(block_panel.shape[:-1] + (3, LMB))]
    convert_element_type x16 -> x0, other arithmetic: 39.4 us -> none  [form_panel(): block_panel.astype(jnp.float32).reshape(block_panel.shape[:-1] + (3, LMB))]
    scatter x16 -> x0, local copies, waits for them, and re-layouts: 39.3 us -> none  [step(): jnp.zeros((row_blocks, CB, width), jnp.float32).at[local]]
    ppermute x0 -> x19, starting transfers between devices: none -> 38.7 us  [the longest x3 17.2 us: body(): lax.ppermute(to_right, 'cam', [(i, i + 1) for i in range(step + 1)])]
    reduce_scatter x1 -> x0, waiting for transfers between devices: 38.2 us -> none  [body(): lax.psum_scatter(result.reshape(row_count, total_blocks * CB), 'cam', sca...]
    dot_general x16 -> x0, matrix products: 36.7 us -> none  [step(): jnp.einsum('rp,kcp->rkc', placed.reshape(row_count, width), block_panel.a...]
  transfers between devices with their start and end apart: 2 -> 19, of which waited for: 2 -> 5; matrix products, arithmetic and copies ran while one was open for 1% -> 1% of each run, Pallas kernels for 0% -> 20%
where the time goes in v3:
time: 84.6 us; the launch traced here: 85.3 us
  starting transfers between devices  38.7 us (46%)
  Pallas kernels  27.8 us (33%)
  waiting for transfers between devices  15.1 us (18%)
  local copies, waits for them, and re-layouts  2.12 us (3%)
  other arithmetic  1.21 us (1%)
    ppermute x3, starting transfers between devices, body(): lax.ppermute(to_right, 'cam', [(i, i + 1) for i in range(step + 1)])  17.2 us
    pallas_call x3, Pallas kernels, sums(): call(functools.partial(kernel, plan), name, outs, scratch(pairs) + more,...  17.2 us
    ppermute x3, starting transfers between devices, body(): lax.ppermute(value, 'cam', [(i, i ^ pos + 1) for i in range(n_cam)])  9.8 us
    ppermute x10, starting transfers between devices, swap(): return lax.ppermute(value, 'lm', [(i, i ^ step) for i in range(n_lm)])  9.08 us
    ppermute x10, waiting for transfers between devices, swap(): return lax.ppermute(value, 'lm', [(i, i ^ step) for i in range(n_lm)])  6.96 us
    ppermute x3, waiting for transfers between devices, body(): lax.ppermute(value, 'cam', [(i, i ^ pos + 1) for i in range(n_cam)])  4.96 us
    ppermute x3, waiting for transfers between devices, body(): lax.ppermute(to_right, 'cam', [(i, i + 1) for i in range(step + 1)])  3.22 us
    ppermute x3, starting transfers between devices, body(): lax.ppermute(to_left, 'cam', [(i, i - 1) for i in range(n_cam - 1 - step,...  2.65 us
  transfers between devices with their start and end apart: 19, of which 5 were waited for; matrix products, arithmetic and copies ran while one was open for 1% of the time, Pallas kernels for 20%

profile of v3, /device:TPU:0, one launch (start us, length us, event | category | flops | bytes accessed | tf_op | source)
XLA Modules:
  0.0 85.3 jit_solution(343451339920584618)
XLA Ops:
  0.0 0.5 collective-permute-start.1
  0.5 0.8 fusion.4
  1.2 0.1 collective-permute-start
  1.3 0.5 collective-permute-start.2
  1.8 0.1 select_reduce_fusion.1.table.refs_0_
  1.9 0.0 copy-start
  1.9 1.4 %copy-done = bf16[2,16,64,384]{3,2,1,0:T(8,128)(2,1)S(1)} copy-done((bf16[2,16,64,384]{3,2,1,0:T(8,128)(2,1)S(1)}, bf16[2,16,64,384]{3,2,1,0:T(8,128)(2,1)}, u32[]{:S(2)}) %copy-start) | copy-done | bytes 1572888
  3.3 0.0 copy-start.1
  3.3 0.7 copy-done.1
  4.0 2.1 %form_own.1 = (bf16[2,1024,768]{2,1,0:T(8,128)(2,1)S(1)}, s32[2,24]{1,0:T(2,128)S(1)}, s32[2,2]{1,0:T(2,128)S(1)}, bf16[2,16,64,384]{3,2,1,0:T(8,128)(2,1)S(1)}) custom-call(s32[2,48]{1,0:T(2,128)S(1)} %select_reduce_fusion.1.table.refs_0_, bf16[2,16,64,384]{3,2,1,0:T(8,128)(2,1)S(1)} %copy-done, f32[3,3,256]{2,1,0:T(4,128)S(1)} %copy-done.1), custom_call_target="tpu_custom_call" | custom-call | tf_op jit(solution)/shard_map/form_own/pallas_call | solution.py:464
  6.2 0.0 collective-permute-done
  6.2 0.1 select_reduce_fusion.table.refs_5_
  6.3 0.0 collective-permute-done.2.cur
  6.3 0.0 collective-permute-done.1.pan.refs_8_
  6.3 2.0 %form_other.1 = (bf16[2,1024,768]{2,1,0:T(8,128)(2,1)S(1)}, s32[2,24]{1,0:T(2,128)S(1)}, s32[2,2]{1,0:T(2,128)S(1)}) custom-call(s32[2,48]{1,0:T(2,128)S(1)} %select_reduce_fusion.table.refs_5_, bf16[2,16,64,384]{3,2,1,0:T(8,128)(2,1)S(1)} %collective-permute-done.1.pan.refs_8_, f32[3,3,256]{2,1,0:T(4,128)S(1)} %collective-permute-done.2.cur), custom_call_target="tpu_custom_call" | custom-call | tf_op jit(solution)/shard_map/form_other/pallas_call | solution.py:472
  8.4 7.2 %send.1 = (s16[272,1536]{1,0:T(8,128)(2,1)S(1)}, s16[272,1536]{1,0:T(8,128)(2,1)S(1)}) custom-call(s32[2,48]{1,0:T(2,128)S(1)} %select_reduce_fusion.1.table.refs_0_, s32[2,24]{1,0:T(2,128)S(1)} %get-tuple-element.35.refs_1_, s32[2,2]{1,0:T(2,128)S(1)} %get-tuple-element.36.refs_2_, bf16[2,16,64,384]{3,2,1,0:T(8,128)(2,1)S(1)} %get-tuple-element.37.refs_3_, ...), custom_call_target="tpu_custom_call" | custom-call | tf_op jit(solution)/shard_map/send/pallas_call | solution.py:489
  15.6 1.7 %collective-permute-start.9 = (s16[272,1536]{1,0:T(8,128)(2,1)S(1)}, s16[272,1536]{1,0:T(8,128)(2,1)S(1)}, u32[]{:S(2)}, u32[]{:S(2)}) collective-permute-start(s16[272,1536]{1,0:T(8,128)(2,1)S(1)} %get-tuple-element.43), channel_id=1, source_target_pairs={{0,16},{4,20},{8,24},{12,28},{16,0},{20,4},{24,8},{28,12},{1,17},{... | collective-permute-start | bytes 2506760 | tf_op jit(solution)/shard_map/ppermute | solution.py:416
  17.4 2.7 %collective-permute-start.3 = (s16[272,1536]{1,0:T(8,128)(2,1)S(1)}, s16[272,1536]{1,0:T(8,128)(2,1)S(1)}, u32[]{:S(2)}, u32[]{:S(2)}) collective-permute-start(s16[272,1536]{1,0:T(8,128)(2,1)S(1)} %get-tuple-element.42), channel_id=1, source_target_pairs={{0,8},{4,12},{8,0},{12,4},{16,24},{20,28},{24,16},{28,20},{1,9},{5... | collective-permute-start | bytes 2506760 | tf_op jit(solution)/shard_map/ppermute | solution.py:416
  20.0 3.8 %chain.1 = (f32[1088,640]{1,0:T(8,128)S(1)}, s16[1040,128]{1,0:T(8,128)(2,1)S(1)}, s16[1040,128]{1,0:T(8,128)(2,1)S(1)}) custom-call(s32[2,48]{1,0:T(2,128)S(1)} %select_reduce_fusion.1.table.refs_0_, s32[2,24]{1,0:T(2,128)S(1)} %get-tuple-element.35.refs_1_, s32[2,2]{1,0:T(2,128)S(1)} %get-tuple-element.36.refs_2_, ...), custom_call_target="tpu_custom_call" | custom-call | tf_op jit(solution)/shard_map/chain/pallas_call | solution.py:489
  23.8 4.3 %collective-permute-start.4 = (s16[1040,128]{1,0:T(8,128)(2,1)S(1)}, s16[1040,128]{1,0:T(8,128)(2,1)S(1)}, u32[]{:S(2)}, u32[]{:S(2)}) collective-permute-start(s16[1040,128]{1,0:T(8,128)(2,1)S(1)} %get-tuple-element.49), channel_id=1, source_target_pairs={{0,1},{4,5},{8,9},{12,13},{16,17},{20,21},{24,25},{28,29}} | collective-permute-start | bytes 798728 | tf_op jit(solution)/shard_map/ppermute | solution.py:528
  28.1 0.7 collective-permute-start.5
  28.8 3.2 %collective-permute-done.4.from_left = s16[1040,128]{1,0:T(8,128)(2,1)S(1)} collective-permute-done((s16[1040,128]{1,0:T(8,128)(2,1)S(1)}, s16[1040,128]{1,0:T(8,128)(2,1)S(1)}, u32[]{:S(2)}, u32[]{:S(2)}) %collective-permute-start.4) | collective-permute-done | bytes 266272 | tf_op jit(solution)/shard_map/ppermute | solution.py:528
  32.0 0.0 collective-permute-done.5.from_right
  32.0 0.6 link.2
  32.5 4.4 %collective-permute-start.6 = (s16[1040,128]{1,0:T(8,128)(2,1)S(1)}, s16[1040,128]{1,0:T(8,128)(2,1)S(1)}, u32[]{:S(2)}, u32[]{:S(2)}) collective-permute-start(s16[1040,128]{1,0:T(8,128)(2,1)S(1)} %get-tuple-element.51), channel_id=1, source_target_pairs={{0,1},{1,2},{4,5},{5,6},{8,9},{9,10},{12,13},{13,14},{16,17},{17,1... | collective-permute-start | bytes 798728 | tf_op jit(solution)/shard_map/ppermute | solution.py:528
  37.0 0.7 collective-permute-start.7
  37.6 6.1 %keep.1 = f32[576,1664]{1,0:T(8,128)S(1)} custom-call(s32[2,48]{1,0:T(2,128)S(1)} %select_reduce_fusion.1.table.refs_0_, s32[2,24]{1,0:T(2,128)S(1)} %get-tuple-element.35.refs_1_, s32[2,2]{1,0:T(2,128)S(1)} %get-tuple-element.36.refs_2_, bf16[2,16,64,384]{3,2,1,0:T(8,128)(2,1)S(1)} %get-tuple-element.37.refs_3_, ...), custom_call_target="tpu_custom_call" | custom-call | tf_op jit(solution)/shard_map/keep/pallas_call | solution.py:489
  43.8 0.0 collective-permute-done.6.from_left
  43.8 0.0 collective-permute-done.7.from_right
  43.8 0.0 collective-permute-done.9.rest_0_.rest_2_
  43.8 0.7 relay.3
  44.5 1.6 %collective-permute-start.10 = (s16[144,1536]{1,0:T(8,128)(2,1)S(1)}, s16[144,1536]{1,0:T(8,128)(2,1)S(1)}, u32[]{:S(2)}, u32[]{:S(2)}) collective-permute-start(s16[144,1536]{1,0:T(8,128)(2,1)S(1)} %relay.3), channel_id=1, source_target_pairs={{0,8},{4,12},{8,0},{12,4},{16,24},{20,28},{24,16},{28,20},{1,9},{5... | collective-permute-start | bytes 1327112 | tf_op jit(solution)/shard_map/ppermute | solution.py:416
  46.1 0.0 collective-permute-done.3.rest_0_
  46.1 0.7 relay.2
  46.8 0.1 collective-permute-start.8
  46.9 0.6 link.3
  47.5 8.5 %collective-permute-start.11 = (s16[1040,128]{1,0:T(8,128)(2,1)S(1)}, s16[1040,128]{1,0:T(8,128)(2,1)S(1)}, u32[]{:S(2)}, u32[]{:S(2)}) collective-permute-start(s16[1040,128]{1,0:T(8,128)(2,1)S(1)} %get-tuple-element.54), channel_id=1, source_target_pairs={{0,1},{1,2},{2,3},{4,5},{5,6},{6,7},{8,9},{9,10},{10,11},{12,13},{... | collective-permute-start | bytes 798728 | tf_op jit(solution)/shard_map/ppermute | solution.py:528
  56.0 1.3 %collective-permute-start.12 = (s16[1040,128]{1,0:T(8,128)(2,1)S(1)}, s16[1040,128]{1,0:T(8,128)(2,1)S(1)}, u32[]{:S(2)}, u32[]{:S(2)}) collective-permute-start(s16[1040,128]{1,0:T(8,128)(2,1)S(1)} %get-tuple-element.55), channel_id=1, source_target_pairs={{1,0},{2,1},{3,2},{5,4},{6,5},{7,6},{9,8},{10,9},{11,10},{13,12},{... | collective-permute-start | bytes 798728 | tf_op jit(solution)/shard_map/ppermute | solution.py:529
  57.3 0.0 collective-permute-done.10.rest_3_
  57.3 0.3 collective-permute-done.8.rest_1_
  57.6 0.9 %cross.1 = (s16[272,384]{1,0:T(8,128)(2,1)S(1)}, s16[272,384]{1,0:T(8,128)(2,1)S(1)}, s16[272,384]{1,0:T(8,128)(2,1)S(1)}) custom-call(f32[576,1664]{1,0:T(8,128)S(1)} %keep.1, s16[272,1536]{1,0:T(8,128)(2,1)S(1)} %collective-permute-done.3.rest_0_, s16[144,1536]{1,0:T(8,128)(2,1)S(1)} %collective-permute-done.8.rest_1_, ...), custom_call_target="tpu_custom_call" | custom-call | tf_op jit(solution)/shard_map/cross/pallas_call | solution.py:565
  58.5 0.0 copy-start.2
  58.5 7.4 %collective-permute-start.16 = (s16[272,384]{1,0:T(8,128)(2,1)S(1)}, s16[272,384]{1,0:T(8,128)(2,1)S(1)}, u32[]{:S(2)}, u32[]{:S(2)}) collective-permute-start(s16[272,384]{1,0:T(8,128)(2,1)S(1)} %get-tuple-element.56), channel_id=1, source_target_pairs={{0,1},{1,0},{2,3},{3,2},{4,5},{5,4},{6,7},{7,6},{8,9},{9,8},{10,11... | collective-permute-start | bytes 626696 | tf_op jit(solution)/shard_map/ppermute | solution.py:573
  65.9 0.0 collective-permute-start.17
  65.9 2.4 %collective-permute-start.18 = (s16[272,384]{1,0:T(8,128)(2,1)S(1)}, s16[272,384]{1,0:T(8,128)(2,1)S(1)}, u32[]{:S(2)}, u32[]{:S(2)}) collective-permute-start(s16[272,384]{1,0:T(8,128)(2,1)S(1)} %get-tuple-element.58), channel_id=1, source_target_pairs={{0,3},{1,2},{2,1},{3,0},{4,7},{5,6},{6,5},{7,4},{8,11},{9,10},{10,... | collective-permute-start | bytes 626696 | tf_op jit(solution)/shard_map/ppermute | solution.py:573
  68.3 0.0 collective-permute-done.11.from_left
  68.3 0.0 collective-permute-done.12.from_right
  68.3 0.3 spread.1
  68.6 0.4 collective-permute-start.13
  69.0 0.0 copy-done.2
  69.0 0.1 pad_maximum_fusion.wide_ref
  69.1 1.0 %collective-permute-start.14 = (s16[272,128]{1,0:T(8,128)(2,1)S(1)}, s16[272,128]{1,0:T(8,128)(2,1)S(1)}, u32[]{:S(2)}, u32[]{:S(2)}) collective-permute-start(s16[272,128]{1,0:T(8,128)(2,1)S(1)} %get-tuple-element.63), channel_id=1, source_target_pairs={{0,16},{4,20},{8,24},{12,28},{16,0},{20,4},{24,8},{28,12},{1,17},{... | collective-permute-start | bytes 208904 | tf_op jit(solution)/shard_map/ppermute | solution.py:416
  70.1 2.9 %collective-permute-done.13.rest_0_ = s16[272,128]{1,0:T(8,128)(2,1)S(1)} collective-permute-done((s16[272,128]{1,0:T(8,128)(2,1)S(1)}, s16[272,128]{1,0:T(8,128)(2,1)S(1)}, u32[]{:S(2)}, u32[]{:S(2)}) %collective-permute-start.13) | collective-permute-done | bytes 69664 | tf_op jit(solution)/shard_map/ppermute | solution.py:416
  73.0 0.7 collective-permute-start.15
  73.6 0.1 pad_add_fusion.me_ref
  73.7 0.7 base.1
  74.4 0.0 collective-permute-done.14.rest_1_
  74.4 3.8 %collective-permute-done.15.rest_2_ = s16[272,128]{1,0:T(8,128)(2,1)S(1)} collective-permute-done((s16[272,128]{1,0:T(8,128)(2,1)S(1)}, s16[272,128]{1,0:T(8,128)(2,1)S(1)}, u32[]{:S(2)}, u32[]{:S(2)}) %collective-permute-start.15) | collective-permute-done | bytes 69664 | tf_op jit(solution)/shard_map/ppermute | solution.py:416
  78.2 0.6 small.1
  78.8 0.0 collective-permute-done.16.rest_0_
  78.8 5.0 %collective-permute-done.17.rest_1_ = s16[272,384]{1,0:T(8,128)(2,1)S(1)} collective-permute-done((s16[272,384]{1,0:T(8,128)(2,1)S(1)}, s16[272,384]{1,0:T(8,128)(2,1)S(1)}, u32[]{:S(2)}, u32[]{:S(2)}) %collective-permute-start.17) | collective-permute-done | bytes 208928 | tf_op jit(solution)/shard_map/ppermute | solution.py:573
  83.8 0.0 collective-permute-done.18.rest_2_
  83.8 1.5 %finish.1 = f32[256,512]{1,0:T(8,128)} custom-call(f32[256,384]{1,0:T(8,128)S(1)} %base.1, f32[256,128]{1,0:T(8,128)S(1)} %small.1, s16[272,384]{1,0:T(8,128)(2,1)S(1)} %collective-permute-done.16.rest_0_, s16[272,384]{1,0:T(8,128)(2,1)S(1)} %collective-permute-done.17.rest_1_, s16[272,384]{1,0:T(8,128)(2,1)S(1)} %collective-permute-done.18.rest_2_), custom_call_target="tpu_custom_call" | custom-call | tf_op jit(solution)/shard_map/finish/pallas_call | solution.py:604
  (2 shorter events, 0.1 us)
Async XLA Ops:
  0.0 6.3 %collective-permute-start.1 = (bf16[2,16,64,384]{3,2,1,0:T(8,128)(2,1)}, bf16[2,16,64,384]{3,2,1,0:T(8,128)(2,1)S(1)}, u32[]{:S(2)}, u32[]{:S(2)}) collective-permute-start(bf16[2,16,64,384]{3,2,1,0:T(8,128)(2,1)} %pan_ref.1), channel_id=1, source_target_pairs={{0,4},{4,0},{8,12},{12,8},{16,20},{20,16},{24,28},{28,24},{1,5},{5... | collective-permute-start | bytes 4718600 | tf_op jit(solution)/shard_map/ppermute | solution.py:416
  1.2 5.0 %collective-permute-start = (s32[2,16]{1,0:T(2,128)S(1)}, s32[2,16]{1,0:T(2,128)S(1)}, u32[]{:S(2)}, u32[]{:S(2)}) collective-permute-start(s32[2,16]{1,0:T(2,128)S(1)} %get-tuple-element.66), channel_id=1, source_target_pairs={{0,4},{4,0},{8,12},{12,8},{16,20},{20,16},{24,28},{28,24},{1,5},{5... | collective-permute-start | bytes 392 | tf_op jit(solution)/shard_map/ppermute | solution.py:416
  1.3 5.0 %collective-permute-start.2 = (f32[3,3,256]{2,1,0:T(4,128)}, f32[3,3,256]{2,1,0:T(4,128)S(1)}, u32[]{:S(2)}, u32[]{:S(2)}) collective-permute-start(f32[3,3,256]{2,1,0:T(4,128)} %cur_ref.1), channel_id=1, source_target_pairs={{0,4},{4,0},{8,12},{12,8},{16,20},{20,16},{24,28},{28,24},{1,5},{5... | collective-permute-start | bytes 27656 | tf_op jit(solution)/shard_map/ppermute | solution.py:416
  1.9 1.4 %copy-start = (bf16[2,16,64,384]{3,2,1,0:T(8,128)(2,1)S(1)}, bf16[2,16,64,384]{3,2,1,0:T(8,128)(2,1)}, u32[]{:S(2)}) copy-start(bf16[2,16,64,384]{3,2,1,0:T(8,128)(2,1)} %pan_ref.1) | copy-start | bytes 4718596
  3.3 0.7 copy-start.1
  15.6 28.2 %collective-permute-start.9 = (s16[272,1536]{1,0:T(8,128)(2,1)S(1)}, s16[272,1536]{1,0:T(8,128)(2,1)S(1)}, u32[]{:S(2)}, u32[]{:S(2)}) collective-permute-start(s16[272,1536]{1,0:T(8,128)(2,1)S(1)} %get-tuple-element.43), channel_id=1, source_target_pairs={{0,16},{4,20},{8,24},{12,28},{16,0},{20,4},{24,8},{28,12},{1,17},{... | collective-permute-start | bytes 2506760 | tf_op jit(solution)/shard_map/ppermute | solution.py:416
  17.4 28.7 %collective-permute-start.3 = (s16[272,1536]{1,0:T(8,128)(2,1)S(1)}, s16[272,1536]{1,0:T(8,128)(2,1)S(1)}, u32[]{:S(2)}, u32[]{:S(2)}) collective-permute-start(s16[272,1536]{1,0:T(8,128)(2,1)S(1)} %get-tuple-element.42), channel_id=1, source_target_pairs={{0,8},{4,12},{8,0},{12,4},{16,24},{20,28},{24,16},{28,20},{1,9},{5... | collective-permute-start | bytes 2506760 | tf_op jit(solution)/shard_map/ppermute | solution.py:416
  23.8 8.2 %collective-permute-start.4 = (s16[1040,128]{1,0:T(8,128)(2,1)S(1)}, s16[1040,128]{1,0:T(8,128)(2,1)S(1)}, u32[]{:S(2)}, u32[]{:S(2)}) collective-permute-start(s16[1040,128]{1,0:T(8,128)(2,1)S(1)} %get-tuple-element.49), channel_id=1, source_target_pairs={{0,1},{4,5},{8,9},{12,13},{16,17},{20,21},{24,25},{28,29}} | collective-permute-start | bytes 798728 | tf_op jit(solution)/shard_map/ppermute | solution.py:528
  28.1 3.9 %collective-permute-start.5 = (s16[1040,128]{1,0:T(8,128)(2,1)S(1)}, s16[1040,128]{1,0:T(8,128)(2,1)S(1)}, u32[]{:S(2)}, u32[]{:S(2)}) collective-permute-start(s16[1040,128]{1,0:T(8,128)(2,1)S(1)} %get-tuple-element.50), channel_id=1, source_target_pairs={{3,2},{7,6},{11,10},{15,14},{19,18},{23,22},{27,26},{31,30}} | collective-permute-start | bytes 798728 | tf_op jit(solution)/shard_map/ppermute | solution.py:529
  32.5 11.3 %collective-permute-start.6 = (s16[1040,128]{1,0:T(8,128)(2,1)S(1)}, s16[1040,128]{1,0:T(8,128)(2,1)S(1)}, u32[]{:S(2)}, u32[]{:S(2)}) collective-permute-start(s16[1040,128]{1,0:T(8,128)(2,1)S(1)} %get-tuple-element.51), channel_id=1, source_target_pairs={{0,1},{1,2},{4,5},{5,6},{8,9},{9,10},{12,13},{13,14},{16,17},{17,1... | collective-permute-start | bytes 798728 | tf_op jit(solution)/shard_map/ppermute | solution.py:528
  37.0 6.9 %collective-permute-start.7 = (s16[1040,128]{1,0:T(8,128)(2,1)S(1)}, s16[1040,128]{1,0:T(8,128)(2,1)S(1)}, u32[]{:S(2)}, u32[]{:S(2)}) collective-permute-start(s16[1040,128]{1,0:T(8,128)(2,1)S(1)} %get-tuple-element.52), channel_id=1, source_target_pairs={{2,1},{3,2},{6,5},{7,6},{10,9},{11,10},{14,13},{15,14},{18,17},{19... | collective-permute-start | bytes 798728 | tf_op jit(solution)/shard_map/ppermute | solution.py:529
  44.5 12.8 %collective-permute-start.10 = (s16[144,1536]{1,0:T(8,128)(2,1)S(1)}, s16[144,1536]{1,0:T(8,128)(2,1)S(1)}, u32[]{:S(2)}, u32[]{:S(2)}) collective-permute-start(s16[144,1536]{1,0:T(8,128)(2,1)S(1)} %relay.3), channel_id=1, source_target_pairs={{0,8},{4,12},{8,0},{12,4},{16,24},{20,28},{24,16},{28,20},{1,9},{5... | collective-permute-start | bytes 1327112 | tf_op jit(solution)/shard_map/ppermute | solution.py:416
  46.8 10.8 %collective-permute-start.8 = (s16[144,1536]{1,0:T(8,128)(2,1)S(1)}, s16[144,1536]{1,0:T(8,128)(2,1)S(1)}, u32[]{:S(2)}, u32[]{:S(2)}) collective-permute-start(s16[144,1536]{1,0:T(8,128)(2,1)S(1)} %relay.2), channel_id=1, source_target_pairs={{0,16},{4,20},{8,24},{12,28},{16,0},{20,4},{24,8},{28,12},{1,17},{... | collective-permute-start | bytes 1327112 | tf_op jit(solution)/shard_map/ppermute | solution.py:416
  47.5 20.9 %collective-permute-start.11 = (s16[1040,128]{1,0:T(8,128)(2,1)S(1)}, s16[1040,128]{1,0:T(8,128)(2,1)S(1)}, u32[]{:S(2)}, u32[]{:S(2)}) collective-permute-start(s16[1040,128]{1,0:T(8,128)(2,1)S(1)} %get-tuple-element.54), channel_id=1, source_target_pairs={{0,1},{1,2},{2,3},{4,5},{5,6},{6,7},{8,9},{9,10},{10,11},{12,13},{... | collective-permute-start | bytes 798728 | tf_op jit(solution)/shard_map/ppermute | solution.py:528
  56.0 12.3 %collective-permute-start.12 = (s16[1040,128]{1,0:T(8,128)(2,1)S(1)}, s16[1040,128]{1,0:T(8,128)(2,1)S(1)}, u32[]{:S(2)}, u32[]{:S(2)}) collective-permute-start(s16[1040,128]{1,0:T(8,128)(2,1)S(1)} %get-tuple-element.55), channel_id=1, source_target_pairs={{1,0},{2,1},{3,2},{5,4},{6,5},{7,6},{9,8},{10,9},{11,10},{13,12},{... | collective-permute-start | bytes 798728 | tf_op jit(solution)/shard_map/ppermute | solution.py:529
  58.5 10.5 %copy-start.2 = (f32[4,64,64]{2,1,0:T(8,128)S(1)}, f32[4,64,64]{2,1,0:T(8,128)}, u32[]{:S(2)}) copy-start(f32[4,64,64]{2,1,0:T(8,128)} %param.9) | copy-start | bytes 196612
  58.5 20.3 %collective-permute-start.16 = (s16[272,384]{1,0:T(8,128)(2,1)S(1)}, s16[272,384]{1,0:T(8,128)(2,1)S(1)}, u32[]{:S(2)}, u32[]{:S(2)}) collective-permute-start(s16[272,384]{1,0:T(8,128)(2,1)S(1)} %get-tuple-element.56), channel_id=1, source_target_pairs={{0,1},{1,0},{2,3},{3,2},{4,5},{5,4},{6,7},{7,6},{8,9},{9,8},{10,11... | collective-permute-start | bytes 626696 | tf_op jit(solution)/shard_map/ppermute | solution.py:573
  65.9 17.9 %collective-permute-start.17 = (s16[272,384]{1,0:T(8,128)(2,1)S(1)}, s16[272,384]{1,0:T(8,128)(2,1)S(1)}, u32[]{:S(2)}, u32[]{:S(2)}) collective-permute-start(s16[272,384]{1,0:T(8,128)(2,1)S(1)} %get-tuple-element.57), channel_id=1, source_target_pairs={{0,2},{1,3},{2,0},{3,1},{4,6},{5,7},{6,4},{7,5},{8,10},{9,11},{10,... | collective-permute-start | bytes 626696 | tf_op jit(solution)/shard_map/ppermute | solution.py:573
  65.9 17.9 %collective-permute-start.18 = (s16[272,384]{1,0:T(8,128)(2,1)S(1)}, s16[272,384]{1,0:T(8,128)(2,1)S(1)}, u32[]{:S(2)}, u32[]{:S(2)}) collective-permute-start(s16[272,384]{1,0:T(8,128)(2,1)S(1)} %get-tuple-element.58), channel_id=1, source_target_pairs={{0,3},{1,2},{2,1},{3,0},{4,7},{5,6},{6,5},{7,4},{8,11},{9,10},{10,... | collective-permute-start | bytes 626696 | tf_op jit(solution)/shard_map/ppermute | solution.py:573
  68.6 4.4 %collective-permute-start.13 = (s16[272,128]{1,0:T(8,128)(2,1)S(1)}, s16[272,128]{1,0:T(8,128)(2,1)S(1)}, u32[]{:S(2)}, u32[]{:S(2)}) collective-permute-start(s16[272,128]{1,0:T(8,128)(2,1)S(1)} %get-tuple-element.62), channel_id=1, source_target_pairs={{0,8},{4,12},{8,0},{12,4},{16,24},{20,28},{24,16},{28,20},{1,9},{5... | collective-permute-start | bytes 208904 | tf_op jit(solution)/shard_map/ppermute | solution.py:416
  69.1 5.3 %collective-permute-start.14 = (s16[272,128]{1,0:T(8,128)(2,1)S(1)}, s16[272,128]{1,0:T(8,128)(2,1)S(1)}, u32[]{:S(2)}, u32[]{:S(2)}) collective-permute-start(s16[272,128]{1,0:T(8,128)(2,1)S(1)} %get-tuple-element.63), channel_id=1, source_target_pairs={{0,16},{4,20},{8,24},{12,28},{16,0},{20,4},{24,8},{28,12},{1,17},{... | collective-permute-start | bytes 208904 | tf_op jit(solution)/shard_map/ppermute | solution.py:416
  73.0 5.2 %collective-permute-start.15 = (s16[272,128]{1,0:T(8,128)(2,1)S(1)}, s16[272,128]{1,0:T(8,128)(2,1)S(1)}, u32[]{:S(2)}, u32[]{:S(2)}) collective-permute-start(s16[272,128]{1,0:T(8,128)(2,1)S(1)} %get-tuple-element.64), channel_id=1, source_target_pairs={{0,24},{4,28},{8,16},{12,20},{16,8},{20,12},{24,0},{28,4},{1,25},{... | collective-permute-start | bytes 208904 | tf_op jit(solution)/shard_map/ppermute | solution.py:416

commit v4 on v3

--- a/solution.py
+++ b/solution.py
@@ -43,8 +43,9 @@
 def encode(dst, lanes, parts):
     blocks = len(parts)
     strip = strip_of(blocks)
-    row = lax.broadcasted_iota(jnp.int32, (strip, LANES), 0)
-    tops = jnp.full((strip, LANES), 2.0**-100, jnp.float32)
+    width = lanes.size
+    row = lax.broadcasted_iota(jnp.int32, (strip, width), 0)
+    tops = jnp.full((strip, width), 2.0**-100, jnp.float32)
     for block, part in enumerate(parts):
         top = jnp.max(jnp.abs(part()), axis=0, keepdims=True)
         tops = jnp.where(row == block, jnp.maximum(top, tops), tops)
@@ -101,30 +102,36 @@
     for region in range(2):
         list_at = region * (region_size + QUAD)
 
-        def one_place(place, count):
-            slot = table[tile, total + region * region_size + place]
-
-            @pl.when(slot >= 0)
-            def form():
-                line_at[tile, list_at + count] = (region * region_size + place) * CB
-                lines = pl.ds(pl.multiple_of((region * region_size + count) * CB, CB), CB)
-                wide = pan[tile, slot].astype(jnp.float32)
-                split = [wide[:, c * LMB : (c + 1) * LMB] for c in range(3)]
-                for q in range(3):
-                    formed = (
-                        split[0] * inverse[0][q]
-                        + split[1] * inverse[1][q]
-                        + split[2] * inverse[2][q]
-                    )
-                    high = formed.astype(jnp.bfloat16)
-                    low = (formed - high.astype(jnp.float32)).astype(jnp.bfloat16)
-                    at = q * LMB
-                    rows[tile, lines, at : at + LMB] = high
-                    rows[tile, lines, WIDTH + at : WIDTH + at + LMB] = low
-
-            return count + jnp.where(slot >= 0, 1, 0)
-
-        count = lax.fori_loop(0, region_size, one_place, jnp.int32(0))
+        def one_form(place, slot, count):
+            line_at[tile, list_at + count] = place * CB
+            lines = pl.ds(pl.multiple_of((region * region_size + count) * CB, CB), CB)
+            wide = pan[tile, slot].astype(jnp.float32)
+            split = [wide[:, c * LMB : (c + 1) * LMB] for c in range(3)]
+            for q in range(3):
+                formed = (
+                    split[0] * inverse[0][q] + split[1] * inverse[1][q] + split[2] * inverse[2][q]
+                )
+                high = formed.astype(jnp.bfloat16)
+                low = (formed - high.astype(jnp.float32)).astype(jnp.bfloat16)
+                at = q * LMB
+                rows[tile, lines, at : at + LMB] = high
+                rows[tile, lines, WIDTH + at : WIDTH + at + LMB] = low
+
+        def some_places(few, count):
+            places = [region * region_size + few * QUAD + place for place in range(QUAD)]
+            slots = [table[tile, total + place] for place in places]
+            counts = [count]
+            for slot in slots:
+                counts.append(counts[-1] + jnp.where(slot >= 0, 1, 0))
+
+            @pl.when(counts[-1] > count)
+            def some():
+                for place, slot, at in zip(places, slots, counts):
+                    pl.when(slot >= 0)(functools.partial(one_form, place, slot, at))
+
+            return counts[-1]
+
+        count = lax.fori_loop(0, region_size // QUAD, some_places, jnp.int32(0))
         many[tile, region] = (count + QUAD - 1) // QUAD
         for extra in range(QUAD):
             line_at[tile, list_at + count + extra] = 2 * region_size * CB
@@ -151,8 +158,13 @@
         form_tile(plan, table, tile, pan, cur, rows, line_at, many)
 
 
+def joint_of(pairs):
+    return 4 if pairs % 4 == 0 and pairs >= 8 else 2
+
+
 def accumulate(plan, sides, right, pair_at, acc):
     base, pairs, regions, region_size = plan
+    joint = joint_of(pairs)
     acc[...] = jnp.zeros_like(acc)
     dump = acc.shape[0] - CB
     for table, line_at, many, pan, rows in sides:
@@ -186,7 +198,8 @@
                     return count + jnp.where(live, 1, 0)
 
                 count = lax.fori_loop(0, pairs, one_pair, jnp.int32(0))
-                pair_at[count] = pairs * LANES
+                for extra in range(joint - 1):
+                    pair_at[count + extra] = pairs * LANES
                 for region in regions:
                     shift = region * region_size * CB if len(regions) == 1 else 0
 
@@ -195,26 +208,26 @@
                         lines = pl.ds(pl.multiple_of(start, QUAD * CB), QUAD * CB)
                         list_at = region * (region_size + QUAD) + group * QUAD
 
-                        def one_dot(double, carry):
-                            first = pl.multiple_of(double * 2 * LANES, 2 * LANES)
+                        def one_dot(few, carry):
+                            first = pl.multiple_of(few * joint * LANES, joint * LANES)
                             result = lax.dot_general(
                                 rows[tile, lines, :],
-                                right[pl.ds(first, 2 * LANES), :],
+                                right[pl.ds(first, joint * LANES), :],
                                 (((1,), (1,)), ((), ())),
                                 preferred_element_type=jnp.float32,
                             )
                             for block in range(QUAD):
                                 line = jnp.minimum(line_at[tile, list_at + block] - shift, dump)
                                 line = pl.multiple_of(line, CB)
-                                for side in range(2):
-                                    lane = pl.multiple_of(pair_at[2 * double + side], LANES)
+                                for side in range(joint):
+                                    lane = pl.multiple_of(pair_at[few * joint + side], LANES)
                                     acc[pl.ds(line, CB), pl.ds(lane, LANES)] += result[
                                         block * CB : (block + 1) * CB,
                                         side * LANES : (side + 1) * LANES,
                                     ]
                             return carry
 
-                        return lax.fori_loop(0, (count + 1) // 2, one_dot, carry)
+                        return lax.fori_loop(0, (count + joint - 1) // joint, one_dot, carry)
 
                     lax.fori_loop(0, many[tile, region], one_group, 0)
 
@@ -223,12 +236,14 @@
         lax.fori_loop(0, rows.shape[0], one_tile, 0)
 
 
-def each_tile(columns, work):
+def each_tile(columns, work, most=4):
+    width = max(w * LANES for w in range(1, most + 1) if columns % (w * LANES) == 0)
+
     def one(start, carry):
-        work(pl.ds(pl.multiple_of(start * LANES, LANES), LANES))
+        work(pl.ds(pl.multiple_of(start * width, width), width))
         return carry
 
-    lax.fori_loop(0, columns // LANES, one, 0)
+    lax.fori_loop(0, columns // width, one, 0)
 
 
 def blocks_at(acc, first, blocks, lanes):
@@ -316,7 +331,7 @@
             parts += given(gathered(keep, rest[:-1], lanes, line, place, blocks))
         encode(dst, lanes, parts)
 
-    each_tile(dst.shape[1], code)
+    each_tile(dst.shape[1], code, 2)
 
 
 def own_rows(firsts, blocks, keep, came, lanes):
@@ -333,13 +348,9 @@
     group = dsts[0].shape[1]
     for other, dst in enumerate(dsts):
 
-        def code(start, carry, other=other, dst=dst):
-            at = pl.multiple_of(start * LANES, LANES)
-            lanes = pl.ds(pl.multiple_of((other + 1) * group + at, LANES), LANES)
-            encode(dst, pl.ds(at, LANES), given(own_rows(firsts, blocks, keep, came, lanes)))
-            return carry
-
-        lax.fori_loop(0, group // LANES, code, 0)
+        for start in range(0, group, LANES):
+            lanes = pl.ds((other + 1) * group + start, LANES)
+            encode(dst, pl.ds(start, LANES), given(own_rows(firsts, blocks, keep, came, lanes)))
 
 
 def hessian_part(me_ref, wide_ref, plan, start, block):
@@ -480,7 +491,7 @@
     def scratch(pairs):
         return [
             pltpu.VMEM(((pairs + 1) * LANES, 2 * WIDTH), jnp.bfloat16),
-            pltpu.SMEM((pairs + 1,), jnp.int32),
+            pltpu.SMEM((pairs + joint_of(pairs),), jnp.int32),
         ]
 
     def sums(kernel, name, base, pairs, regions, outs, more, tables):
@@ -529,6 +540,8 @@
         from_right = lax.ppermute(
             to_left, "cam", [(i, i - 1) for i in range(n_cam - 1 - step, n_cam)]
         )
+        if not links:
+            from_left, from_right = lax.optimization_barrier((from_left, from_right, keep))[:2]
         links.append((from_left, from_right))
         if step < n_cam - 2:
             groups = (n_cam - 2 - step, step + 2)
@@ -548,7 +561,7 @@
         size = chips >> (stage + 1)
         if size == 1:
             break
-        keep_now = lax.optimization_barrier((keep, links[min(n_cam - 3, 1)]))[0]
+        keep_now = lax.optimization_barrier((keep, links[0]))[0]
         sends = [
             call(
                 functools.partial(relay_kernel, (firsts[half], half_blocks, size)),

time: 84.6 us -> 78.1 us (0.923)
  starting transfers between devices: 38.7 us -> 32.7 us
  Pallas kernels: 27.8 us -> 22.5 us
  waiting for transfers between devices: 15.1 us -> 19.6 us
    ppermute x3, waiting for transfers between devices: 0.01 us -> 6.16 us  [body(): lax.ppermute(to_left, 'cam', [(i, i - 1) for i in range(n_cam - 1 - step,...]
    ppermute x3, starting transfers between devices: 9.8 us -> 5.56 us  [body(): lax.ppermute(value, 'cam', [(i, i ^ pos + 1) for i in range(n_cam)])]
    pallas_call x3, Pallas kernels: 17.2 us -> 13.2 us  [sums(): call(functools.partial(kernel, plan), name, outs, scratch(pairs) + more,...]
    ppermute x3, starting transfers between devices: 17.2 us -> 13.9 us  [body(): lax.ppermute(to_right, 'cam', [(i, i + 1) for i in range(step + 1)])]
    ppermute x3, waiting for transfers between devices: 4.96 us -> 1.78 us  [body(): lax.ppermute(value, 'cam', [(i, i ^ pos + 1) for i in range(n_cam)])]
    ppermute x3, waiting for transfers between devices: 3.22 us -> 5.63 us  [body(): lax.ppermute(to_right, 'cam', [(i, i + 1) for i in range(step + 1)])]
    ppermute x10, starting transfers between devices: 9.08 us -> 10.5 us  [swap(): return lax.ppermute(value, 'lm', [(i, i ^ step) for i in range(n_lm)])]
    ppermute x10, waiting for transfers between devices: 6.96 us -> 6.03 us  [swap(): return lax.ppermute(value, 'lm', [(i, i ^ step) for i in range(n_lm)])]
  transfers between devices with their start and end apart: 19 -> 19, of which waited for: 5 -> 7; matrix products, arithmetic and copies ran while one was open for 1% -> 2% of each run, Pallas kernels for 20% -> 17%
where the time goes in v4:
time: 78.1 us; the launch traced here: 78.4 us
  starting transfers between devices  32.7 us (42%)
  Pallas kernels  22.5 us (29%)
  waiting for transfers between devices  19.6 us (25%)
  local copies, waits for them, and re-layouts  2.12 us (3%)
  other arithmetic  1.21 us (2%)
    ppermute x3, starting transfers between devices, body(): lax.ppermute(to_right, 'cam', [(i, i + 1) for i in range(step + 1)])  13.9 us
    pallas_call x3, Pallas kernels, sums(): call(functools.partial(kernel, plan), name, outs, scratch(pairs) + more,...  13.2 us
    ppermute x10, starting transfers between devices, swap(): return lax.ppermute(value, 'lm', [(i, i ^ step) for i in range(n_lm)])  10.5 us
    ppermute x3, waiting for transfers between devices, body(): lax.ppermute(to_left, 'cam', [(i, i - 1) for i in range(n_cam - 1 - step,...  6.16 us
    ppermute x10, waiting for transfers between devices, swap(): return lax.ppermute(value, 'lm', [(i, i ^ step) for i in range(n_lm)])  6.03 us
    ppermute x3, waiting for transfers between devices, body(): lax.ppermute(to_right, 'cam', [(i, i + 1) for i in range(step + 1)])  5.63 us
    ppermute x3, starting transfers between devices, body(): lax.ppermute(value, 'cam', [(i, i ^ pos + 1) for i in range(n_cam)])  5.56 us
    ppermute x3, starting transfers between devices, body(): lax.ppermute(to_left, 'cam', [(i, i - 1) for i in range(n_cam - 1 - step,...  2.65 us
  transfers between devices with their start and end apart: 19, of which 7 were waited for; matrix products, arithmetic and copies ran while one was open for 2% of the time, Pallas kernels for 17%

profile of v4, /device:TPU:0, one launch (start us, length us, event | category | flops | bytes accessed | tf_op | source)
XLA Modules:
  0.0 78.4 jit_solution(7005840504358876601)
XLA Ops:
  0.0 0.5 collective-permute-start.1
  0.5 0.8 fusion.4
  1.2 0.1 collective-permute-start
  1.3 0.5 collective-permute-start.2
  1.8 0.1 select_reduce_fusion.1.table.refs_0_
  1.9 0.0 copy-start
  1.9 1.4 %copy-done = bf16[2,16,64,384]{3,2,1,0:T(8,128)(2,1)S(1)} copy-done((bf16[2,16,64,384]{3,2,1,0:T(8,128)(2,1)S(1)}, bf16[2,16,64,384]{3,2,1,0:T(8,128)(2,1)}, u32[]{:S(2)}) %copy-start) | copy-done | bytes 1572888
  3.3 0.0 copy-start.1
  3.3 0.7 copy-done.1
  4.0 1.9 %form_own.1 = (bf16[2,1024,768]{2,1,0:T(8,128)(2,1)S(1)}, s32[2,24]{1,0:T(2,128)S(1)}, s32[2,2]{1,0:T(2,128)S(1)}, bf16[2,16,64,384]{3,2,1,0:T(8,128)(2,1)S(1)}) custom-call(s32[2,48]{1,0:T(2,128)S(1)} %select_reduce_fusion.1.table.refs_0_, bf16[2,16,64,384]{3,2,1,0:T(8,128)(2,1)S(1)} %copy-done, f32[3,3,256]{2,1,0:T(4,128)S(1)} %copy-done.1), custom_call_target="tpu_custom_call" | custom-call | tf_op jit(solution)/shard_map/form_own/pallas_call | solution.py:475
  6.0 0.0 collective-permute-done
  6.0 0.1 select_reduce_fusion.table.refs_5_
  6.1 0.0 collective-permute-done.2.cur
  6.1 0.0 collective-permute-done.1.pan.refs_8_
  6.1 1.6 %form_other.1 = (bf16[2,1024,768]{2,1,0:T(8,128)(2,1)S(1)}, s32[2,24]{1,0:T(2,128)S(1)}, s32[2,2]{1,0:T(2,128)S(1)}) custom-call(s32[2,48]{1,0:T(2,128)S(1)} %select_reduce_fusion.table.refs_5_, bf16[2,16,64,384]{3,2,1,0:T(8,128)(2,1)S(1)} %collective-permute-done.1.pan.refs_8_, f32[3,3,256]{2,1,0:T(4,128)S(1)} %collective-permute-done.2.cur), custom_call_target="tpu_custom_call" | custom-call | tf_op jit(solution)/shard_map/form_other/pallas_call | solution.py:483
  7.7 5.9 %send.1 = (s16[272,1536]{1,0:T(8,128)(2,1)S(1)}, s16[272,1536]{1,0:T(8,128)(2,1)S(1)}) custom-call(s32[2,48]{1,0:T(2,128)S(1)} %select_reduce_fusion.1.table.refs_0_, s32[2,24]{1,0:T(2,128)S(1)} %get-tuple-element.37.refs_1_, s32[2,2]{1,0:T(2,128)S(1)} %get-tuple-element.38.refs_2_, bf16[2,16,64,384]{3,2,1,0:T(8,128)(2,1)S(1)} %get-tuple-element.39.refs_3_, ...), custom_call_target="tpu_custom_call" | custom-call | tf_op jit(solution)/shard_map/send/pallas_call | solution.py:500
  13.7 0.1 collective-permute-start.7
  13.8 4.4 %collective-permute-start.3 = (s16[272,1536]{1,0:T(8,128)(2,1)S(1)}, s16[272,1536]{1,0:T(8,128)(2,1)S(1)}, u32[]{:S(2)}, u32[]{:S(2)}) collective-permute-start(s16[272,1536]{1,0:T(8,128)(2,1)S(1)} %get-tuple-element.44), channel_id=1, source_target_pairs={{0,8},{4,12},{8,0},{12,4},{16,24},{20,28},{24,16},{28,20},{1,9},{5... | collective-permute-start | bytes 2506760 | tf_op jit(solution)/shard_map/ppermute | solution.py:427
  18.2 3.7 %chain.1 = (f32[1088,640]{1,0:T(8,128)S(1)}, s16[1040,128]{1,0:T(8,128)(2,1)S(1)}, s16[1040,128]{1,0:T(8,128)(2,1)S(1)}) custom-call(s32[2,48]{1,0:T(2,128)S(1)} %select_reduce_fusion.1.table.refs_0_, s32[2,24]{1,0:T(2,128)S(1)} %get-tuple-element.37.refs_1_, s32[2,2]{1,0:T(2,128)S(1)} %get-tuple-element.38.refs_2_, ...), custom_call_target="tpu_custom_call" | custom-call | tf_op jit(solution)/shard_map/chain/pallas_call | solution.py:500
  21.9 4.1 %collective-permute-start.4 = (s16[1040,128]{1,0:T(8,128)(2,1)S(1)}, s16[1040,128]{1,0:T(8,128)(2,1)S(1)}, u32[]{:S(2)}, u32[]{:S(2)}) collective-permute-start(s16[1040,128]{1,0:T(8,128)(2,1)S(1)} %get-tuple-element.51), channel_id=1, source_target_pairs={{0,1},{4,5},{8,9},{12,13},{16,17},{20,21},{24,25},{28,29}} | collective-permute-start | bytes 798728 | tf_op jit(solution)/shard_map/ppermute | solution.py:539
  26.0 0.7 collective-permute-start.5
  26.7 3.5 %keep.1 = f32[576,1664]{1,0:T(8,128)S(1)} custom-call(s32[2,48]{1,0:T(2,128)S(1)} %select_reduce_fusion.1.table.refs_0_, s32[2,24]{1,0:T(2,128)S(1)} %get-tuple-element.37.refs_1_, s32[2,2]{1,0:T(2,128)S(1)} %get-tuple-element.38.refs_2_, bf16[2,16,64,384]{3,2,1,0:T(8,128)(2,1)S(1)} %get-tuple-element.39.refs_3_, ...), custom_call_target="tpu_custom_call" | custom-call | tf_op jit(solution)/shard_map/keep/pallas_call | solution.py:500
  30.2 2.5 %collective-permute-done.4.from_left = s16[1040,128]{1,0:T(8,128)(2,1)S(1)} collective-permute-done((s16[1040,128]{1,0:T(8,128)(2,1)S(1)}, s16[1040,128]{1,0:T(8,128)(2,1)S(1)}, u32[]{:S(2)}, u32[]{:S(2)}) %collective-permute-start.4) | collective-permute-done | bytes 266272 | tf_op jit(solution)/shard_map/ppermute | solution.py:539
  32.7 0.0 collective-permute-done.5.from_right
  32.8 0.6 link.2
  33.3 0.7 collective-permute-start.10
  34.0 5.0 %collective-permute-start.9 = (s16[1040,128]{1,0:T(8,128)(2,1)S(1)}, s16[1040,128]{1,0:T(8,128)(2,1)S(1)}, u32[]{:S(2)}, u32[]{:S(2)}) collective-permute-start(s16[1040,128]{1,0:T(8,128)(2,1)S(1)} %get-tuple-element.56), channel_id=1, source_target_pairs={{0,1},{1,2},{4,5},{5,6},{8,9},{9,10},{12,13},{13,14},{16,17},{17,1... | collective-permute-start | bytes 798728 | tf_op jit(solution)/shard_map/ppermute | solution.py:539
  39.0 0.0 collective-permute-done.7.rest_0_.rest_2_
  39.0 0.5 relay.3
  39.5 0.1 collective-permute-start.8
  39.6 0.0 collective-permute-done.3.rest_0_
  39.6 0.5 relay.2
  40.1 1.8 %collective-permute-start.6 = (s16[144,1536]{1,0:T(8,128)(2,1)S(1)}, s16[144,1536]{1,0:T(8,128)(2,1)S(1)}, u32[]{:S(2)}, u32[]{:S(2)}) collective-permute-start(s16[144,1536]{1,0:T(8,128)(2,1)S(1)} %relay.2), channel_id=1, source_target_pairs={{0,16},{4,20},{8,24},{12,28},{16,0},{20,4},{24,8},{28,12},{1,17},{... | collective-permute-start | bytes 1327112 | tf_op jit(solution)/shard_map/ppermute | solution.py:427
  41.8 0.0 collective-permute-done.10.from_right
  41.8 3.1 %collective-permute-done.9.from_left = s16[1040,128]{1,0:T(8,128)(2,1)S(1)} collective-permute-done((s16[1040,128]{1,0:T(8,128)(2,1)S(1)}, s16[1040,128]{1,0:T(8,128)(2,1)S(1)}, u32[]{:S(2)}, u32[]{:S(2)}) %collective-permute-start.9) | collective-permute-done | bytes 266272 | tf_op jit(solution)/shard_map/ppermute | solution.py:539
  44.9 0.6 link.3
  45.5 4.9 %collective-permute-start.11 = (s16[1040,128]{1,0:T(8,128)(2,1)S(1)}, s16[1040,128]{1,0:T(8,128)(2,1)S(1)}, u32[]{:S(2)}, u32[]{:S(2)}) collective-permute-start(s16[1040,128]{1,0:T(8,128)(2,1)S(1)} %get-tuple-element.58), channel_id=1, source_target_pairs={{0,1},{1,2},{2,3},{4,5},{5,6},{6,7},{8,9},{9,10},{10,11},{12,13},{... | collective-permute-start | bytes 798728 | tf_op jit(solution)/shard_map/ppermute | solution.py:539
  50.4 1.3 %collective-permute-start.12 = (s16[1040,128]{1,0:T(8,128)(2,1)S(1)}, s16[1040,128]{1,0:T(8,128)(2,1)S(1)}, u32[]{:S(2)}, u32[]{:S(2)}) collective-permute-start(s16[1040,128]{1,0:T(8,128)(2,1)S(1)} %get-tuple-element.59), channel_id=1, source_target_pairs={{1,0},{2,1},{3,2},{5,4},{6,5},{7,6},{9,8},{10,9},{11,10},{13,12},{... | collective-permute-start | bytes 798728 | tf_op jit(solution)/shard_map/ppermute | solution.py:540
  51.7 0.0 collective-permute-done.8.rest_3_
  51.7 0.5 collective-permute-done.6.rest_1_
  52.2 0.7 cross.1
  52.9 0.0 copy-start.2
  52.9 2.8 %collective-permute-start.16 = (s16[272,384]{1,0:T(8,128)(2,1)S(1)}, s16[272,384]{1,0:T(8,128)(2,1)S(1)}, u32[]{:S(2)}, u32[]{:S(2)}) collective-permute-start(s16[272,384]{1,0:T(8,128)(2,1)S(1)} %get-tuple-element.60), channel_id=1, source_target_pairs={{0,1},{1,0},{2,3},{3,2},{4,5},{5,4},{6,7},{7,6},{8,9},{9,8},{10,11... | collective-permute-start | bytes 626696 | tf_op jit(solution)/shard_map/ppermute | solution.py:586
  55.8 1.3 %collective-permute-start.17 = (s16[272,384]{1,0:T(8,128)(2,1)S(1)}, s16[272,384]{1,0:T(8,128)(2,1)S(1)}, u32[]{:S(2)}, u32[]{:S(2)}) collective-permute-start(s16[272,384]{1,0:T(8,128)(2,1)S(1)} %get-tuple-element.61), channel_id=1, source_target_pairs={{0,2},{1,3},{2,0},{3,1},{4,6},{5,7},{6,4},{7,5},{8,10},{9,11},{10,... | collective-permute-start | bytes 626696 | tf_op jit(solution)/shard_map/ppermute | solution.py:586
  57.1 1.4 %collective-permute-start.18 = (s16[272,384]{1,0:T(8,128)(2,1)S(1)}, s16[272,384]{1,0:T(8,128)(2,1)S(1)}, u32[]{:S(2)}, u32[]{:S(2)}) collective-permute-start(s16[272,384]{1,0:T(8,128)(2,1)S(1)} %get-tuple-element.62), channel_id=1, source_target_pairs={{0,3},{1,2},{2,1},{3,0},{4,7},{5,6},{6,5},{7,4},{8,11},{9,10},{10,... | collective-permute-start | bytes 626696 | tf_op jit(solution)/shard_map/ppermute | solution.py:586
  58.5 0.0 collective-permute-done.11.from_left
  58.5 6.2 %collective-permute-done.12.from_right = s16[1040,128]{1,0:T(8,128)(2,1)S(1)} collective-permute-done((s16[1040,128]{1,0:T(8,128)(2,1)S(1)}, s16[1040,128]{1,0:T(8,128)(2,1)S(1)}, u32[]{:S(2)}, u32[]{:S(2)}) %collective-permute-start.12) | collective-permute-done | bytes 266272 | tf_op jit(solution)/shard_map/ppermute | solution.py:540
  64.7 0.3 spread.1
  64.9 0.1 collective-permute-start.13
  65.0 0.0 copy-done.2
  65.0 0.1 pad_maximum_fusion.wide_ref
  65.1 1.9 %collective-permute-start.14 = (s16[272,128]{1,0:T(8,128)(2,1)S(1)}, s16[272,128]{1,0:T(8,128)(2,1)S(1)}, u32[]{:S(2)}, u32[]{:S(2)}) collective-permute-start(s16[272,128]{1,0:T(8,128)(2,1)S(1)} %get-tuple-element.67), channel_id=1, source_target_pairs={{0,16},{4,20},{8,24},{12,28},{16,0},{20,4},{24,8},{28,12},{1,17},{... | collective-permute-start | bytes 208904 | tf_op jit(solution)/shard_map/ppermute | solution.py:427
  67.0 2.3 %collective-permute-done.13.rest_0_ = s16[272,128]{1,0:T(8,128)(2,1)S(1)} collective-permute-done((s16[272,128]{1,0:T(8,128)(2,1)S(1)}, s16[272,128]{1,0:T(8,128)(2,1)S(1)}, u32[]{:S(2)}, u32[]{:S(2)}) %collective-permute-start.13) | collective-permute-done | bytes 69664 | tf_op jit(solution)/shard_map/ppermute | solution.py:427
  69.3 1.3 %collective-permute-start.15 = (s16[272,128]{1,0:T(8,128)(2,1)S(1)}, s16[272,128]{1,0:T(8,128)(2,1)S(1)}, u32[]{:S(2)}, u32[]{:S(2)}) collective-permute-start(s16[272,128]{1,0:T(8,128)(2,1)S(1)} %get-tuple-element.68), channel_id=1, source_target_pairs={{0,24},{4,28},{8,16},{12,20},{16,8},{20,12},{24,0},{28,4},{1,25},{... | collective-permute-start | bytes 208904 | tf_op jit(solution)/shard_map/ppermute | solution.py:427
  70.6 0.1 pad_add_fusion.me_ref
  70.6 0.7 base.1
  71.3 0.0 collective-permute-done.14.rest_1_
  71.3 3.2 %collective-permute-done.15.rest_2_ = s16[272,128]{1,0:T(8,128)(2,1)S(1)} collective-permute-done((s16[272,128]{1,0:T(8,128)(2,1)S(1)}, s16[272,128]{1,0:T(8,128)(2,1)S(1)}, u32[]{:S(2)}, u32[]{:S(2)}) %collective-permute-start.15) | collective-permute-done | bytes 69664 | tf_op jit(solution)/shard_map/ppermute | solution.py:427
  74.5 0.6 small.1
  75.1 0.0 collective-permute-done.16.rest_0_
  75.1 1.8 %collective-permute-done.17.rest_1_ = s16[272,384]{1,0:T(8,128)(2,1)S(1)} collective-permute-done((s16[272,384]{1,0:T(8,128)(2,1)S(1)}, s16[272,384]{1,0:T(8,128)(2,1)S(1)}, u32[]{:S(2)}, u32[]{:S(2)}) %collective-permute-start.17) | collective-permute-done | bytes 208928 | tf_op jit(solution)/shard_map/ppermute | solution.py:586
  76.9 0.0 collective-permute-done.18.rest_2_
  76.9 1.5 %finish.1 = f32[256,512]{1,0:T(8,128)} custom-call(f32[256,384]{1,0:T(8,128)S(1)} %base.1, f32[256,128]{1,0:T(8,128)S(1)} %small.1, s16[272,384]{1,0:T(8,128)(2,1)S(1)} %collective-permute-done.16.rest_0_, s16[272,384]{1,0:T(8,128)(2,1)S(1)} %collective-permute-done.17.rest_1_, s16[272,384]{1,0:T(8,128)(2,1)S(1)} %collective-permute-done.18.rest_2_), custom_call_target="tpu_custom_call" | custom-call | tf_op jit(solution)/shard_map/finish/pallas_call | solution.py:617
  (2 shorter events, 0.1 us)
Async XLA Ops:
  0.0 6.1 %collective-permute-start.1 = (bf16[2,16,64,384]{3,2,1,0:T(8,128)(2,1)}, bf16[2,16,64,384]{3,2,1,0:T(8,128)(2,1)S(1)}, u32[]{:S(2)}, u32[]{:S(2)}) collective-permute-start(bf16[2,16,64,384]{3,2,1,0:T(8,128)(2,1)} %pan_ref.1), channel_id=1, source_target_pairs={{0,4},{4,0},{8,12},{12,8},{16,20},{20,16},{24,28},{28,24},{1,5},{5... | collective-permute-start | bytes 4718600 | tf_op jit(solution)/shard_map/ppermute | solution.py:427
  1.2 4.8 %collective-permute-start = (s32[2,16]{1,0:T(2,128)S(1)}, s32[2,16]{1,0:T(2,128)S(1)}, u32[]{:S(2)}, u32[]{:S(2)}) collective-permute-start(s32[2,16]{1,0:T(2,128)S(1)} %get-tuple-element.70), channel_id=1, source_target_pairs={{0,4},{4,0},{8,12},{12,8},{16,20},{20,16},{24,28},{28,24},{1,5},{5... | collective-permute-start | bytes 392 | tf_op jit(solution)/shard_map/ppermute | solution.py:427
  1.3 4.8 %collective-permute-start.2 = (f32[3,3,256]{2,1,0:T(4,128)}, f32[3,3,256]{2,1,0:T(4,128)S(1)}, u32[]{:S(2)}, u32[]{:S(2)}) collective-permute-start(f32[3,3,256]{2,1,0:T(4,128)} %cur_ref.1), channel_id=1, source_target_pairs={{0,4},{4,0},{8,12},{12,8},{16,20},{20,16},{24,28},{28,24},{1,5},{5... | collective-permute-start | bytes 27656 | tf_op jit(solution)/shard_map/ppermute | solution.py:427
  1.9 1.4 %copy-start = (bf16[2,16,64,384]{3,2,1,0:T(8,128)(2,1)S(1)}, bf16[2,16,64,384]{3,2,1,0:T(8,128)(2,1)}, u32[]{:S(2)}) copy-start(bf16[2,16,64,384]{3,2,1,0:T(8,128)(2,1)} %pan_ref.1) | copy-start | bytes 4718596
  3.3 0.7 copy-start.1
  13.7 25.4 %collective-permute-start.7 = (s16[272,1536]{1,0:T(8,128)(2,1)S(1)}, s16[272,1536]{1,0:T(8,128)(2,1)S(1)}, u32[]{:S(2)}, u32[]{:S(2)}) collective-permute-start(s16[272,1536]{1,0:T(8,128)(2,1)S(1)} %get-tuple-element.45), channel_id=1, source_target_pairs={{0,16},{4,20},{8,24},{12,28},{16,0},{20,4},{24,8},{28,12},{1,17},{... | collective-permute-start | bytes 2506760 | tf_op jit(solution)/shard_map/ppermute | solution.py:427
  13.8 25.8 %collective-permute-start.3 = (s16[272,1536]{1,0:T(8,128)(2,1)S(1)}, s16[272,1536]{1,0:T(8,128)(2,1)S(1)}, u32[]{:S(2)}, u32[]{:S(2)}) collective-permute-start(s16[272,1536]{1,0:T(8,128)(2,1)S(1)} %get-tuple-element.44), channel_id=1, source_target_pairs={{0,8},{4,12},{8,0},{12,4},{16,24},{20,28},{24,16},{28,20},{1,9},{5... | collective-permute-start | bytes 2506760 | tf_op jit(solution)/shard_map/ppermute | solution.py:427
  21.9 10.8 %collective-permute-start.4 = (s16[1040,128]{1,0:T(8,128)(2,1)S(1)}, s16[1040,128]{1,0:T(8,128)(2,1)S(1)}, u32[]{:S(2)}, u32[]{:S(2)}) collective-permute-start(s16[1040,128]{1,0:T(8,128)(2,1)S(1)} %get-tuple-element.51), channel_id=1, source_target_pairs={{0,1},{4,5},{8,9},{12,13},{16,17},{20,21},{24,25},{28,29}} | collective-permute-start | bytes 798728 | tf_op jit(solution)/shard_map/ppermute | solution.py:539
  26.0 6.8 %collective-permute-start.5 = (s16[1040,128]{1,0:T(8,128)(2,1)S(1)}, s16[1040,128]{1,0:T(8,128)(2,1)S(1)}, u32[]{:S(2)}, u32[]{:S(2)}) collective-permute-start(s16[1040,128]{1,0:T(8,128)(2,1)S(1)} %get-tuple-element.52), channel_id=1, source_target_pairs={{3,2},{7,6},{11,10},{15,14},{19,18},{23,22},{27,26},{31,30}} | collective-permute-start | bytes 798728 | tf_op jit(solution)/shard_map/ppermute | solution.py:540
  33.3 8.5 %collective-permute-start.10 = (s16[1040,128]{1,0:T(8,128)(2,1)S(1)}, s16[1040,128]{1,0:T(8,128)(2,1)S(1)}, u32[]{:S(2)}, u32[]{:S(2)}) collective-permute-start(s16[1040,128]{1,0:T(8,128)(2,1)S(1)} %get-tuple-element.57), channel_id=1, source_target_pairs={{2,1},{3,2},{6,5},{7,6},{10,9},{11,10},{14,13},{15,14},{18,17},{19... | collective-permute-start | bytes 798728 | tf_op jit(solution)/shard_map/ppermute | solution.py:540
  34.0 10.9 %collective-permute-start.9 = (s16[1040,128]{1,0:T(8,128)(2,1)S(1)}, s16[1040,128]{1,0:T(8,128)(2,1)S(1)}, u32[]{:S(2)}, u32[]{:S(2)}) collective-permute-start(s16[1040,128]{1,0:T(8,128)(2,1)S(1)} %get-tuple-element.56), channel_id=1, source_target_pairs={{0,1},{1,2},{4,5},{5,6},{8,9},{9,10},{12,13},{13,14},{16,17},{17,1... | collective-permute-start | bytes 798728 | tf_op jit(solution)/shard_map/ppermute | solution.py:539
  39.5 12.2 %collective-permute-start.8 = (s16[144,1536]{1,0:T(8,128)(2,1)S(1)}, s16[144,1536]{1,0:T(8,128)(2,1)S(1)}, u32[]{:S(2)}, u32[]{:S(2)}) collective-permute-start(s16[144,1536]{1,0:T(8,128)(2,1)S(1)} %relay.3), channel_id=1, source_target_pairs={{0,8},{4,12},{8,0},{12,4},{16,24},{20,28},{24,16},{28,20},{1,9},{5... | collective-permute-start | bytes 1327112 | tf_op jit(solution)/shard_map/ppermute | solution.py:427
  40.1 12.1 %collective-permute-start.6 = (s16[144,1536]{1,0:T(8,128)(2,1)S(1)}, s16[144,1536]{1,0:T(8,128)(2,1)S(1)}, u32[]{:S(2)}, u32[]{:S(2)}) collective-permute-start(s16[144,1536]{1,0:T(8,128)(2,1)S(1)} %relay.2), channel_id=1, source_target_pairs={{0,16},{4,20},{8,24},{12,28},{16,0},{20,4},{24,8},{28,12},{1,17},{... | collective-permute-start | bytes 1327112 | tf_op jit(solution)/shard_map/ppermute | solution.py:427
  45.5 13.0 %collective-permute-start.11 = (s16[1040,128]{1,0:T(8,128)(2,1)S(1)}, s16[1040,128]{1,0:T(8,128)(2,1)S(1)}, u32[]{:S(2)}, u32[]{:S(2)}) collective-permute-start(s16[1040,128]{1,0:T(8,128)(2,1)S(1)} %get-tuple-element.58), channel_id=1, source_target_pairs={{0,1},{1,2},{2,3},{4,5},{5,6},{6,7},{8,9},{9,10},{10,11},{12,13},{... | collective-permute-start | bytes 798728 | tf_op jit(solution)/shard_map/ppermute | solution.py:539
  50.4 14.3 %collective-permute-start.12 = (s16[1040,128]{1,0:T(8,128)(2,1)S(1)}, s16[1040,128]{1,0:T(8,128)(2,1)S(1)}, u32[]{:S(2)}, u32[]{:S(2)}) collective-permute-start(s16[1040,128]{1,0:T(8,128)(2,1)S(1)} %get-tuple-element.59), channel_id=1, source_target_pairs={{1,0},{2,1},{3,2},{5,4},{6,5},{7,6},{9,8},{10,9},{11,10},{13,12},{... | collective-permute-start | bytes 798728 | tf_op jit(solution)/shard_map/ppermute | solution.py:540
  52.9 12.1 %copy-start.2 = (f32[4,64,64]{2,1,0:T(8,128)S(1)}, f32[4,64,64]{2,1,0:T(8,128)}, u32[]{:S(2)}) copy-start(f32[4,64,64]{2,1,0:T(8,128)} %param.9) | copy-start | bytes 196612
  52.9 22.2 %collective-permute-start.16 = (s16[272,384]{1,0:T(8,128)(2,1)S(1)}, s16[272,384]{1,0:T(8,128)(2,1)S(1)}, u32[]{:S(2)}, u32[]{:S(2)}) collective-permute-start(s16[272,384]{1,0:T(8,128)(2,1)S(1)} %get-tuple-element.60), channel_id=1, source_target_pairs={{0,1},{1,0},{2,3},{3,2},{4,5},{5,4},{6,7},{7,6},{8,9},{9,8},{10,11... | collective-permute-start | bytes 626696 | tf_op jit(solution)/shard_map/ppermute | solution.py:586
  55.8 21.2 %collective-permute-start.17 = (s16[272,384]{1,0:T(8,128)(2,1)S(1)}, s16[272,384]{1,0:T(8,128)(2,1)S(1)}, u32[]{:S(2)}, u32[]{:S(2)}) collective-permute-start(s16[272,384]{1,0:T(8,128)(2,1)S(1)} %get-tuple-element.61), channel_id=1, source_target_pairs={{0,2},{1,3},{2,0},{3,1},{4,6},{5,7},{6,4},{7,5},{8,10},{9,11},{10,... | collective-permute-start | bytes 626696 | tf_op jit(solution)/shard_map/ppermute | solution.py:586
  57.1 19.8 %collective-permute-start.18 = (s16[272,384]{1,0:T(8,128)(2,1)S(1)}, s16[272,384]{1,0:T(8,128)(2,1)S(1)}, u32[]{:S(2)}, u32[]{:S(2)}) collective-permute-start(s16[272,384]{1,0:T(8,128)(2,1)S(1)} %get-tuple-element.62), channel_id=1, source_target_pairs={{0,3},{1,2},{2,1},{3,0},{4,7},{5,6},{6,5},{7,4},{8,11},{9,10},{10,... | collective-permute-start | bytes 626696 | tf_op jit(solution)/shard_map/ppermute | solution.py:586
  64.9 4.4 %collective-permute-start.13 = (s16[272,128]{1,0:T(8,128)(2,1)S(1)}, s16[272,128]{1,0:T(8,128)(2,1)S(1)}, u32[]{:S(2)}, u32[]{:S(2)}) collective-permute-start(s16[272,128]{1,0:T(8,128)(2,1)S(1)} %get-tuple-element.66), channel_id=1, source_target_pairs={{0,8},{4,12},{8,0},{12,4},{16,24},{20,28},{24,16},{28,20},{1,9},{5... | collective-permute-start | bytes 208904 | tf_op jit(solution)/shard_map/ppermute | solution.py:427
  65.1 6.2 %collective-permute-start.14 = (s16[272,128]{1,0:T(8,128)(2,1)S(1)}, s16[272,128]{1,0:T(8,128)(2,1)S(1)}, u32[]{:S(2)}, u32[]{:S(2)}) collective-permute-start(s16[272,128]{1,0:T(8,128)(2,1)S(1)} %get-tuple-element.67), channel_id=1, source_target_pairs={{0,16},{4,20},{8,24},{12,28},{16,0},{20,4},{24,8},{28,12},{1,17},{... | collective-permute-start | bytes 208904 | tf_op jit(solution)/shard_map/ppermute | solution.py:427
  69.3 5.2 %collective-permute-start.15 = (s16[272,128]{1,0:T(8,128)(2,1)S(1)}, s16[272,128]{1,0:T(8,128)(2,1)S(1)}, u32[]{:S(2)}, u32[]{:S(2)}) collective-permute-start(s16[272,128]{1,0:T(8,128)(2,1)S(1)} %get-tuple-element.68), channel_id=1, source_target_pairs={{0,24},{4,28},{8,16},{12,20},{16,8},{20,12},{24,0},{28,4},{1,25},{... | collective-permute-start | bytes 208904 | tf_op jit(solution)/shard_map/ppermute | solution.py:427
